TPU v7x, 128 devices: a whole 4x4x4 slice. The times are simulated.
128 devices in a mesh: seq: 64 (over y, z, x_hi, core), head: 2 (over x_lo).
Axes of the slice: x: 4 (x_hi: 2, x_lo: 2; x = x_hi * 2 + x_lo), y: 4, z: 4, core: 2. Of those that a mesh axis runs over, the one named last changes fastest.
Arguments:
- tokens: bfloat16 [16384, 2048], P('seq'), may hold values from -24 to 24
- w_query: bfloat16 [2048, 2048], P(None, 'head'), may hold values from -1 to 1
- w_key: bfloat16 [2048, 2048], P(None, 'head'), may hold values from -1 to 1
- w_value: bfloat16 [2048, 2048], P(None, 'head'), may hold values from -0.125 to 0.125
- w_out: bfloat16 [2048, 2048], P('head'), may hold values from -0.125 to 0.125
- cotangent: bfloat16 [16384, 2048], P('seq', 'head'), may hold values from -6 to 6
Outputs:
- mixed: bfloat16 [16384, 2048], P('seq', 'head')
- input_grad: bfloat16 [16384, 2048], P('seq', 'head')
All inputs are finite; a program needn't handle non-finite values.
Results may differ from a plain program's by a relative error of at most 0.013.
The roundings to bfloat16 on the way count: a program that leaves them out, or rounds other values in their place, can miss the bound.
Values may be sent and summed in bfloat16 or wider, within the bound.
A program may use at most 128 MiB of HBM per device.

v0:
```python
import math

import jax
import jax.numpy as jnp
from jax import lax
from jax.experimental import pallas as pl
from jax.experimental.pallas import tpu as pltpu
from jax.sharding import PartitionSpec as P

MESH = pl.DeviceIdType.MESH
F32 = jnp.float32
BF16 = jnp.bfloat16
LN2 = math.log(2.0)
SCALE = 1.0 / math.sqrt(128)

TOK = 256
WID = 512
HALF = 1024
L1, L2, L3, YP = 0, 128, 256, 384
ROWS = 640


def level_region(dz, dx):
    return (L2 + dx * 64, 64) if dz == 1 else (L3 + (dz - 2) * 64 + dx * 32, 32)


def plane_region(dz, dx):
    return (YP + (dz * 2 + dx) * 32, 32)


def dot(a, b):
    return jnp.dot(a, b, preferred_element_type=F32)


def dot_t(a, b):
    return lax.dot_general(a, b, (((1,), (1,)), ((), ())), preferred_element_type=F32)


def pool(value):
    n = value.shape[0]
    out = lax.broadcasted_iota(jnp.int32, (n // 2, n), 0)
    inp = lax.broadcasted_iota(jnp.int32, (n // 2, n), 1)
    return dot(jnp.where(inp // 2 == out, 0.5, 0.0).astype(BF16), value).astype(BF16)


def spread(value):
    n = value.shape[0]
    out = lax.broadcasted_iota(jnp.int32, (2 * n, n), 0)
    inp = lax.broadcasted_iota(jnp.int32, (2 * n, n), 1)
    return dot(jnp.where(out // 2 == inp, 0.5, 0.0).astype(BF16), value.astype(BF16))


def t_dot(a, b):
    return lax.dot_general(a, b, (((0,), (0,)), ((), ())), preferred_element_type=F32)


def lanes(i, width):
    return pl.ds(pl.multiple_of(i * width, width), width)


(
    M_TOK0, M_TOK1, M_COTC, M_COTH, M_COTF, M_MIXC, M_MIXH, M_INC, M_INH,
    M_Y, M_X1, M_X2, M_ZO, M_ZW, M_ZX, M_ZY,
    B_X1, B_XA, B_Z, B_ZY, B_Y, N_MSG,
) = (0, 1, 2, 3, 4, 5, 6, 7, 8, 9, 12, 13, 14, 17, 20, 23, 26, 27, 28, 34, 40, 43)


def kernel(
    tok_h, wq_h, wk_h, wv_h, wo_h, cot_h, mix_o, ing_o,
    tok, w, wo, cot, kv, qb, go, p0, p1, p2, p3, p4, wpl, p2x, p3x, ybuf, S,
    pf, E, inv, GP, ypb, att, acc, c_send, c_recv, h_send, h_recv, ic_recv, ih_recv,
    dkv, dp0, dS, sb, RS, xa_s, xa_r, gy_s, gy_r, dq, gk, out_b,
    lsem, ssem, rsem,
):
    s = lax.axis_index("seq")
    hd = lax.axis_index("head")
    c = s % 2

    def flip(bit):
        return (1 - 2 * ((s // bit) % 2)) * bit

    core = (s + flip(1), hd)
    head = (s, 1 - hd)
    xhi = (s + flip(2), hd)
    zdev = {1: (s + flip(4), hd), 2: (s + flip(8), hd), 3: (s + flip(4) + flip(8), hd)}
    ydev = {1: (s + flip(16), hd), 2: (s + flip(32), hd), 3: (s + flip(16) + flip(32), hd)}

    own = pl.ds(pl.multiple_of(hd * HALF, HALF), HALF)
    oth = pl.ds(pl.multiple_of((1 - hd) * HALF, HALF), HALF)
    wcol = pl.ds(pl.multiple_of(c * WID, WID), WID)
    halves = ((own, pl.ds(0, HALF)), (oth, pl.ds(HALF, HALF)))
    lcount = [0]

    def load(src, dst):
        cp = pltpu.make_async_copy(src, dst, lsem.at[lcount[0]])
        lcount[0] += 1
        cp.start()
        return cp

    ld_tok = [load(tok_h.at[:, a], tok.at[pl.ds(0, TOK), b]) for a, b in halves]
    ld_k = [load(wk_h.at[a, wcol], w.at[b, pl.ds(0, WID)]) for a, b in halves]
    ld_v = [load(wv_h.at[a, wcol], w.at[b, pl.ds(WID, WID)]) for a, b in halves]
    ld_q = [load(wq_h.at[a, wcol], w.at[b, pl.ds(2 * WID, WID)]) for a, b in halves]
    ld_cot = load(cot_h, cot.at[pl.ds(0, TOK), pl.ds(0, HALF)])
    ld_o = [load(wo_h.at[wcol, a], wo.at[:, b]) for a, b in halves]

    barrier = pltpu.get_barrier_semaphore()
    partners = [core, head, xhi] + [zdev[k] for k in (1, 2, 3)] + [ydev[k] for k in (1, 2, 3)]
    for d in partners:
        pl.semaphore_signal(barrier, inc=1, device_id=d, device_id_type=MESH)
    pl.semaphore_wait(barrier, len(partners))

    def send(n, src, dst, dev):
        cp = pltpu.make_async_remote_copy(
            src_ref=src, dst_ref=dst, send_sem=ssem.at[n], recv_sem=rsem.at[n],
            device_id=dev, device_id_type=MESH,
        )
        cp.start()
        return cp

    def rows(ref, region):
        return ref.at[pl.ds(*region)]

    s_tok = [
        send(M_TOK0 + i, tok_h.at[:, a], tok.at[pl.ds(TOK, TOK), b], core)
        for i, (a, b) in enumerate(halves)
    ]
    s_cotc = send(M_COTC, cot_h, cot.at[pl.ds(TOK, TOK), pl.ds(0, HALF)], core)
    s_coth = send(M_COTH, cot_h, cot.at[pl.ds(0, TOK), pl.ds(HALF, HALF)], head)

    for cp in ld_tok + ld_k + ld_v:
        cp.wait()

    def kv_tiles(b):
        def body(j, _):
            r = dot(tok[pl.ds(b * TOK, TOK), :], w[:, lanes(j, 256)]).astype(BF16)
            kv[pl.ds(b * TOK, TOK), lanes(j, 256)] = r
            return 0

        lax.fori_loop(0, 4, body, 0)

    kv_tiles(0)
    for cp in s_tok:
        cp.wait_recv()
    kv_tiles(1)

    for b in range(2):
        p0[pl.ds(b * 128, 128), :] = pool(kv[pl.ds(b * TOK, TOK), :])
    p1[...] = pool(p0[...])
    m_x1 = send(M_X1, p1, rows(S, (L1, 128)), xhi)
    p2[...] = pool(p1[...])
    m_zo = [send(M_ZO, p2, rows(S, level_region(1, 0)), zdev[1])]
    p3[...] = pool(p2[...])
    m_zo += [send(M_ZO + k - 1, p3, rows(S, level_region(k, 0)), zdev[k]) for k in (2, 3)]
    p4[...] = pool(p3[...])
    m_y = [send(M_Y + k - 1, p4, ybuf.at[k - 1], ydev[k]) for k in (1, 2, 3)]

    for cp in ld_q:
        cp.wait()

    def q_body(j, _):
        qb[:, lanes(j, 256)] = dot(tok[...], w[:, pl.ds(pl.multiple_of(2 * WID + j * 256, 256), 256)]).astype(BF16)
        return 0

    lax.fori_loop(0, 2, q_body, 0)

    for cp in m_y:
        cp.wait_recv()
    wpl[pl.ds(0, 16), :] = ybuf[0]
    wpl[pl.ds(16, 16), :] = pool(jnp.concatenate([ybuf[1], ybuf[2]], axis=0))
    m_x2 = send(M_X2, wpl, rows(S, plane_region(0, 1)), xhi)
    m_zw = [send(M_ZW + k - 1, wpl, rows(S, plane_region(k, 0)), zdev[k]) for k in (1, 2, 3)]
    S[pl.ds(*plane_region(0, 0)), :] = wpl[...]

    m_x1.wait_recv()
    p2x[...] = pool(S[pl.ds(L1, 128), :])
    m_zx = [send(M_ZX, p2x, rows(S, level_region(1, 1)), zdev[1])]
    p3x[...] = pool(p2x[...])
    m_zx += [send(M_ZX + k - 1, p3x, rows(S, level_region(k, 1)), zdev[k]) for k in (2, 3)]
    m_x2.wait_recv()
    m_zy = [
        send(M_ZY + k - 1, rows(S, plane_region(0, 1)), rows(S, plane_region(k, 1)), zdev[k])
        for k in (1, 2, 3)
    ]

    s_coth.wait_recv()
    s_cotf = send(
        M_COTF, cot.at[pl.ds(0, TOK), pl.ds(HALF, HALF)], cot.at[pl.ds(TOK, TOK), pl.ds(HALF, HALF)], core
    )
    ld_cot.wait()
    for cp in ld_o:
        cp.wait()

    def go_tiles(b):
        def body(j, _):
            go[pl.ds(b * TOK, TOK), lanes(j, 256)] = dot_t(
                cot[pl.ds(b * TOK, TOK), :], wo[lanes(j, 256), :]
            ).astype(BF16)
            return 0

        lax.fori_loop(0, 2, body, 0)

    go_tiles(0)
    s_cotc.wait_recv()
    s_cotf.wait_recv()
    go_tiles(1)

    r_iota = lax.broadcasted_iota(jnp.int32, (256, 256), 0)
    ypb[...] = jnp.where((r_iota // 16) % 2 == 0, 5 * LN2, 6 * LN2).astype(F32)

    for cp in m_zo + m_zw + m_zx + m_zy:
        cp.wait_recv()

    chunks = [
        (0, 256, 0.0), (256, 128, LN2), (384 + L1, 128, 2 * LN2), (384 + L2, 128, 3 * LN2),
        (384 + L3, 128, 4 * LN2), (384 + YP, 256, None),
    ]

    def source(first, size, b, h, value):
        col = pl.ds(pl.multiple_of(h * 128 + value * WID, 128), 128)
        if first == 0:
            return kv[pl.ds(b * TOK, TOK), col]
        if first == 256:
            return p0[pl.ds((1 - b) * 128, 128), col]
        return S[pl.ds(first - 384, size), col]

    def forward(h, _):
        hcol = lanes(h, 128)
        for b in range(2):
            q = qb[pl.ds(b * TOK, TOK), hcol]
            it = h * 2 + b
            peak = None
            for first, size, bias in chunks:
                l = dot_t(source(first, size, b, h, 0), q) * SCALE
                if bias is None:
                    l = l + ypb[...]
                elif bias:
                    l = l + bias
                E[it, pl.ds(first, size), :] = l
                top = jnp.max(l, axis=0, keepdims=True)
                peak = top if peak is None else jnp.maximum(peak, top)
            total = None
            for first, size, bias in chunks:
                e = jnp.exp(E[it, pl.ds(first, size), :] - peak)
                E[it, pl.ds(first, size), :] = e
                part = jnp.sum(e, axis=0, keepdims=True)
                total = part if total is None else total + part
            scale = 1.0 / total
            inv[it] = jnp.broadcast_to(scale, (8, 256))
            a = None
            for first, size, bias in chunks:
                pb = (E[it, pl.ds(first, size), :] * scale).astype(BF16)
                part = t_dot(source(first, size, b, h, 1), pb)
                a = part if a is None else a + part
            att[pl.ds(b * TOK, TOK), hcol] = a.T.astype(BF16)
        return 0

    lax.fori_loop(0, 4, forward, 0)

    def out_tiles(j, _):
        acc[:, lanes(j, 256)] = dot(att[...], wo[:, lanes(j, 256)])
        c_send[:, lanes(j, 256)] = acc[pl.ds(TOK, TOK), lanes(j, 256)].astype(BF16)
        return 0

    lax.fori_loop(0, 8, out_tiles, 0)
    s_mixc = send(M_MIXC, c_send, c_recv, core)

    def backward(h, _):
        hcol = lanes(h, 128)
        vcol = pl.ds(pl.multiple_of(h * 128 + WID, 128), 128)
        for b in range(2):
            q = qb[pl.ds(b * TOK, TOK), hcol]
            g = go[pl.ds(b * TOK, TOK), hcol]
            it = h * 2 + b
            scale = inv[it][0:1, :]
            rd = None
            for first, size, bias in chunks:
                gp = dot_t(source(first, size, b, h, 1), g)
                GP[pl.ds(first, size), :] = gp
                p = E[it, pl.ds(first, size), :] * scale
                E[it, pl.ds(first, size), :] = p
                part = jnp.sum(p * gp, axis=0, keepdims=True)
                rd = part if rd is None else rd + part
            dqt = None
            for first, size, bias in chunks:
                p = E[it, pl.ds(first, size), :]
                dl = (p * (GP[pl.ds(first, size), :] - rd) * SCALE).astype(BF16)
                dvv = dot(p.astype(BF16), g)
                dkk = dot(dl, q)
                part = t_dot(source(first, size, b, h, 0), dl)
                dqt = part if dqt is None else dqt + part
                if first == 0:
                    dkv[pl.ds(b * TOK, TOK), hcol] = dkk
                    dkv[pl.ds(b * TOK, TOK), vcol] = dvv
                elif first == 256:
                    dp0[pl.ds((1 - b) * 128, 128), hcol] = dkk
                    dp0[pl.ds((1 - b) * 128, 128), vcol] = dvv
                elif b == 0:
                    dS[pl.ds(first - 384, size), hcol] = dkk
                    dS[pl.ds(first - 384, size), vcol] = dvv
                else:
                    dkk = dkk + dS[pl.ds(first - 384, size), hcol]
                    dvv = dvv + dS[pl.ds(first - 384, size), vcol]
                    dS[pl.ds(first - 384, size), hcol] = dkk
                    dS[pl.ds(first - 384, size), vcol] = dvv
                    sb[pl.ds(first - 384, size), hcol] = dkk.astype(BF16)
                    sb[pl.ds(first - 384, size), vcol] = dvv.astype(BF16)
            dq[pl.ds(b * TOK, TOK), hcol] = dqt.T.astype(BF16)
        return 0

    lax.fori_loop(0, 4, backward, 0)

    b_z, b_zy = {}, {}
    for dx in (1, 0):
        for k in (1, 2, 3):
            r = level_region(k, dx)
            b_z[k, dx] = send(B_Z + 2 * (k - 1) + dx, rows(sb, r), rows(RS, r), zdev[k])
            r = plane_region(k, dx)
            b_zy[k, dx] = send(B_ZY + 2 * (k - 1) + dx, rows(sb, r), rows(RS, r), zdev[k])
        if dx == 1:
            b_x1 = send(B_X1, rows(sb, (L1, 128)), rows(RS, (L1, 128)), xhi)

    s_mixc.wait_recv()

    def mix_tiles(j, _):
        h_send[:, lanes(j, 256)] = (
            acc[pl.ds(0, TOK), pl.ds(pl.multiple_of(HALF + j * 256, 256), 256)]
            + c_recv[:, pl.ds(pl.multiple_of(HALF + j * 256, 256), 256)].astype(F32)
        ).astype(BF16)
        return 0

    lax.fori_loop(0, 4, mix_tiles, 0)
    s_mixh = send(M_MIXH, h_send, h_recv, head)

    def collect(dx):
        for k in (1, 2, 3):
            b_z[k, dx].wait_recv()
            b_zy[k, dx].wait_recv()
        low = RS[pl.ds(*level_region(2, dx)), :].astype(F32) + RS[pl.ds(*level_region(3, dx)), :].astype(F32)
        top = spread(low) + RS[pl.ds(*level_region(1, dx)), :].astype(F32)
        plane = dS[pl.ds(*plane_region(0, dx)), :]
        for k in (1, 2, 3):
            plane = plane + RS[pl.ds(*plane_region(k, dx)), :].astype(F32)
        return top, plane

    top, plane = collect(1)
    xa_s[pl.ds(0, 64), :] = top.astype(BF16)
    xa_s[pl.ds(64, 32), :] = plane.astype(BF16)
    b_xa = send(B_XA, xa_s, xa_r, xhi)
    top, plane = collect(0)
    pf[pl.ds(0, 64), :] = top
    pf[pl.ds(64, 32), :] = plane

    s_mixh.wait_recv()

    def mix_last(j, _):
        out_b[:, lanes(j, 256)] = (
            acc[pl.ds(0, TOK), lanes(j, 256)]
            + c_recv[:, lanes(j, 256)].astype(F32)
            + h_recv[:, lanes(j, 256)].astype(F32)
        ).astype(BF16)
        return 0

    lax.fori_loop(0, 4, mix_last, 0)
    st_mix = load(out_b, mix_o)

    b_xa.wait_recv()
    top = pf[pl.ds(0, 64), :] + xa_r[pl.ds(0, 64), :].astype(F32)
    plane = pf[pl.ds(64, 32), :] + xa_r[pl.ds(64, 32), :].astype(F32)
    gy_s[0] = plane[0:16].astype(BF16)
    high = spread(plane[16:32])
    gy_s[1] = high[0:16].astype(BF16)
    gy_s[2] = high[16:32].astype(BF16)
    b_y = [send(B_Y + k - 1, gy_s.at[k - 1], gy_r.at[k - 1], ydev[k]) for k in (1, 2, 3)]

    def in_q(j, _):
        acc[:, lanes(j, 256)] = dot_t(dq[...], w[lanes(j, 256), pl.ds(2 * WID, WID)])
        return 0

    lax.fori_loop(0, 8, in_q, 0)

    for cp in b_y:
        cp.wait_recv()
    b_x1.wait_recv()
    g4 = gy_r[0].astype(F32) + gy_r[1].astype(F32) + gy_r[2].astype(F32)
    top = top + spread(spread(g4))
    low = spread(top) + RS[pl.ds(L1, 128), :].astype(F32)
    low = spread(low) + dp0[...]
    for b in range(2):
        gk[pl.ds(b * TOK, TOK), :] = (
            spread(low[b * 128 : (b + 1) * 128]) + dkv[pl.ds(b * TOK, TOK), :]
        ).astype(BF16)

    s_mixc.wait_send()

    def in_tiles(j, _):
        acc[:, lanes(j, 256)] += dot_t(gk[...], w[lanes(j, 256), pl.ds(0, 2 * WID)])
        c_send[:, lanes(j, 256)] = acc[pl.ds(TOK, TOK), lanes(j, 256)].astype(BF16)
        return 0

    lax.fori_loop(0, 8, in_tiles, 0)
    s_inc = send(M_INC, c_send, ic_recv, core)
    s_mixh.wait_send()
    s_inc.wait_recv()

    def inh_tiles(j, _):
        h_send[:, lanes(j, 256)] = (
            acc[pl.ds(0, TOK), pl.ds(pl.multiple_of(HALF + j * 256, 256), 256)]
            + ic_recv[:, pl.ds(pl.multiple_of(HALF + j * 256, 256), 256)].astype(F32)
        ).astype(BF16)
        return 0

    lax.fori_loop(0, 4, inh_tiles, 0)
    s_inh = send(M_INH, h_send, ih_recv, head)
    st_mix.wait()
    s_inh.wait_recv()

    def in_last(j, _):
        out_b[:, lanes(j, 256)] = (
            acc[pl.ds(0, TOK), lanes(j, 256)]
            + ic_recv[:, lanes(j, 256)].astype(F32)
            + ih_recv[:, lanes(j, 256)].astype(F32)
        ).astype(BF16)
        return 0

    lax.fori_loop(0, 4, in_last, 0)
    st_in = load(out_b, ing_o)

    for cp in s_tok + [s_cotc, s_coth, s_cotf, m_x1, m_x2, b_x1, b_xa, s_inc, s_inh]:
        cp.wait_send()
    for cp in m_y + m_zo + m_zw + m_zx + m_zy + b_y + list(b_z.values()) + list(b_zy.values()):
        cp.wait_send()
    st_in.wait()


def per_device(tokens, w_query, w_key, w_value, w_out, cotangent):
    V = pltpu.VMEM
    scratch = [
        V((2 * TOK, 2 * HALF), BF16),
        V((2 * HALF, 3 * WID), BF16),
        V((WID, 2 * HALF), BF16),
        V((2 * TOK, 2 * HALF), BF16),
        V((2 * TOK, 2 * WID), BF16),
        V((2 * TOK, WID), BF16),
        V((2 * TOK, WID), BF16),
        V((256, 2 * WID), BF16),
        V((128, 2 * WID), BF16),
        V((64, 2 * WID), BF16),
        V((32, 2 * WID), BF16),
        V((16, 2 * WID), BF16),
        V((32, 2 * WID), BF16),
        V((64, 2 * WID), BF16),
        V((32, 2 * WID), BF16),
        V((3, 16, 2 * WID), BF16),
        V((ROWS, 2 * WID), BF16),
        V((96, 2 * WID), F32),
        V((8, 1024, 256), F32),
        V((8, 8, 256), F32),
        V((1024, 256), F32),
        V((256, 256), F32),
        V((2 * TOK, WID), BF16),
        V((2 * TOK, 2 * HALF), F32),
        V((TOK, 2 * HALF), BF16),
        V((TOK, 2 * HALF), BF16),
        V((TOK, HALF), BF16),
        V((TOK, HALF), BF16),
        V((TOK, 2 * HALF), BF16),
        V((TOK, HALF), BF16),
        V((2 * TOK, 2 * WID), F32),
        V((256, 2 * WID), F32),
        V((ROWS, 2 * WID), F32),
        V((ROWS, 2 * WID), BF16),
        V((ROWS, 2 * WID), BF16),
        V((96, 2 * WID), BF16),
        V((96, 2 * WID), BF16),
        V((3, 16, 2 * WID), BF16),
        V((3, 16, 2 * WID), BF16),
        V((2 * TOK, WID), BF16),
        V((2 * TOK, 2 * WID), BF16),
        V((TOK, HALF), BF16),
        pltpu.SemaphoreType.DMA((16,)),
        pltpu.SemaphoreType.DMA((N_MSG,)),
        pltpu.SemaphoreType.DMA((N_MSG,)),
    ]
    any_spec = pl.BlockSpec(memory_space=pl.ANY)
    out = jax.ShapeDtypeStruct((TOK, HALF), BF16)
    return pl.pallas_call(
        kernel,
        out_shape=(out, out),
        in_specs=[any_spec] * 6,
        out_specs=(any_spec, any_spec),
        scratch_shapes=scratch,
        compiler_params=pltpu.CompilerParams(
            collective_id=0, has_side_effects=True, vmem_limit_bytes=60 * 2**20
        ),
    )(tokens, w_query, w_key, w_value, w_out, cotangent)


def solution(mesh):
    return jax.shard_map(
        per_device,
        mesh=mesh,
        in_specs=(
            P("seq", None), P(None, "head"), P(None, "head"), P(None, "head"),
            P("head", None), P("seq", "head"),
        ),
        out_specs=(P("seq", "head"), P("seq", "head")),
        check_vma=False,
    )
```

profile of v0, /device:TPU:1, one launch (start us, length us, event | category | flops | bytes accessed | tf_op | source)
XLA Modules:
  0.0 102.4 jit_solution(8284980754800717477)
XLA Ops:
  0.6 98.1 %shard_map.77 = (bf16[256,1024]{1,0:T(8,128)(2,1)}, bf16[256,1024]{1,0:T(8,128)(2,1)}) custom-call(bf16[256,2048]{1,0:T(8,128)(2,1)} %tok_h.1, bf16[2048,1024]{1,0:T(8,128)(2,1)} %wq_h.1, bf16[2048,1024]{1,0:T(8,128)(2,1)} %wk_h.1, bf16[2048,1024]{1,0:T(8,128)(2,1)} %wv_h.1, bf16[1024,2048]{1,0:T(8,128)(2,1)} %wo_h.1, bf16[256,1024]{1,0:T(8,128)(2,1)} %cot_h.1), custom_call_target="tpu_custom_call" | custom-call | tf_op jit(solution)/shard_map/pallas_call | solution.py:487
  98.7 1.9 %copy.10 = bf16[256,1024]{1,0:T(8,128)(2,1)} copy(bf16[256,1024]{1,0:T(8,128)(2,1)} %get-tuple-element.4) | data formatting | bytes 1048576
  100.6 1.9 %copy.11 = bf16[256,1024]{1,0:T(8,128)(2,1)} copy(bf16[256,1024]{1,0:T(8,128)(2,1)} %get-tuple-element.5) | data formatting | bytes 1048576
where the time goes:
time: 103 us; the launch traced here: 102 us
  Pallas kernels  98.1 us (95%)
  local copies, waits for them, and re-layouts  3.74 us (4%)
    pallas_call x1, Pallas kernels, per_device(): pl.pallas_call(kernel, out_shape=(out, out), in_specs=[any_spec] * 6, out...  98.1 us
    unnamed x2, local copies, waits for them, and re-layouts  3.74 us

commit v1 on v0

v1 whole, which is shorter than its diff:
```python
import math

import jax
import jax.numpy as jnp
from jax import lax
from jax.experimental import pallas as pl
from jax.experimental.pallas import tpu as pltpu
from jax.sharding import PartitionSpec as P

MESH = pl.DeviceIdType.MESH
F32 = jnp.float32
BF16 = jnp.bfloat16
LN2 = math.log(2.0)
SCALE = 1.0 / math.sqrt(128)

TOK = 256
WID = 512
HALF = 1024
ROWS = 640


def level_region(dz, dx):
    return (128 + dx * 256, 64) if dz == 1 else (128 + dx * 256 + 32 * dz, 32)


def plane_region(dz, dx):
    return (256 + dx * 256 + 32 * dz, 32)


def dot(a, b):
    return jnp.dot(a, b, preferred_element_type=F32)


def dot_t(a, b):
    return lax.dot_general(a, b, (((1,), (1,)), ((), ())), preferred_element_type=F32)


def pool(value):
    n = value.shape[0]
    out = lax.broadcasted_iota(jnp.int32, (n // 2, n), 0)
    inp = lax.broadcasted_iota(jnp.int32, (n // 2, n), 1)
    return dot(jnp.where(inp // 2 == out, 0.5, 0.0).astype(BF16), value).astype(BF16)


def spread(value):
    n = value.shape[0]
    out = lax.broadcasted_iota(jnp.int32, (2 * n, n), 0)
    inp = lax.broadcasted_iota(jnp.int32, (2 * n, n), 1)
    return dot(jnp.where(out // 2 == inp, 0.5, 0.0).astype(BF16), value.astype(BF16))


def t_dot(a, b):
    return lax.dot_general(a, b, (((0,), (0,)), ((), ())), preferred_element_type=F32)


def lanes(i, width):
    return pl.ds(pl.multiple_of(i * width, width), width)


(
    M_TOK, M_COTC, M_COTH, M_COTF, M_MIXC, M_MIXH, M_INC, M_INH,
    M_Y, M_X1, M_X2, M_ZO, M_ZW, M_ZX, M_ZY,
    B_X1, B_XA, B_Z, B_ZY, B_Y, M_LC, M_LH, N_MSG,
) = (0, 2, 3, 5, 7, 11, 13, 17, 19, 22, 23, 24, 27, 30, 33, 36, 37, 38, 44, 50, 53, 57, 59)


def kernel(
    tok_h, wq_h, wk_h, wv_h, wo_h, cot_h, mix_o, ing_o,
    tok, w, wo, cot, kv, qb, go, p0, p1, p2, p3, p4, wpl, p2x, p3x, ybuf, S,
    pf, E, stat, fin, GP, ypb, att, acc, macc, c_send, c_recv, h_send, h_recv, ic_recv, ih_send, ih_recv,
    lacc, lc_send, lc_recv, lh_send, lh_recv,
    dkv, dp0, dS, sb, RS, xa_s, xa_r, gy_s, gy_r, dq, gk, out_b,
    lsem, ssem, rsem,
):
    s = lax.axis_index("seq")
    hd = lax.axis_index("head")
    c = s % 2

    def flip(bit):
        return (1 - 2 * ((s // bit) % 2)) * bit

    core = (s + flip(1), hd)
    head = (s, 1 - hd)
    xhi = (s + flip(2), hd)
    zdev = {1: (s + flip(4), hd), 2: (s + flip(8), hd), 3: (s + flip(4) + flip(8), hd)}
    ydev = {1: (s + flip(16), hd), 2: (s + flip(32), hd), 3: (s + flip(16) + flip(32), hd)}

    own = pl.ds(pl.multiple_of(hd * HALF, HALF), HALF)
    oth = pl.ds(pl.multiple_of((1 - hd) * HALF, HALF), HALF)
    wcol = pl.ds(pl.multiple_of(c * WID, WID), WID)
    halves = ((own, pl.ds(0, HALF)), (oth, pl.ds(HALF, HALF)))
    lcount = [0]

    def load(src, dst):
        cp = pltpu.make_async_copy(src, dst, lsem.at[lcount[0]])
        lcount[0] += 1
        cp.start()
        return cp

    ld_tok = [load(tok_h.at[:, a], tok.at[pl.ds(0, TOK), b]) for a, b in halves]
    ld_k = [load(wk_h.at[a, wcol], w.at[b, pl.ds(0, WID)]) for a, b in halves]
    ld_v = [load(wv_h.at[a, wcol], w.at[b, pl.ds(WID, WID)]) for a, b in halves]
    ld_q = [load(wq_h.at[a, wcol], w.at[b, pl.ds(2 * WID, WID)]) for a, b in halves]
    ld_cot = load(cot_h, cot.at[pl.ds(0, TOK), pl.ds(0, HALF)])
    ld_o = [load(wo_h.at[wcol, a], wo.at[:, b]) for a, b in halves]

    barrier = pltpu.get_barrier_semaphore()
    partners = [core, head, xhi] + [zdev[k] for k in (1, 2, 3)] + [ydev[k] for k in (1, 2, 3)]
    for d in partners:
        pl.semaphore_signal(barrier, inc=1, device_id=d, device_id_type=MESH)
    pl.semaphore_wait(barrier, len(partners))

    def send(n, src, dst, dev):
        cp = pltpu.make_async_remote_copy(
            src_ref=src, dst_ref=dst, send_sem=ssem.at[n], recv_sem=rsem.at[n],
            device_id=dev, device_id_type=MESH,
        )
        cp.start()
        return cp

    def rows(ref, region):
        return ref.at[pl.ds(*region)]

    s_tok = [
        send(M_TOK + i, tok_h.at[:, a], tok.at[pl.ds(TOK, TOK), b], core)
        for i, (a, b) in enumerate(halves)
    ]
    s_cotc = send(M_COTC, cot_h, cot.at[pl.ds(TOK, TOK), pl.ds(0, HALF)], core)

    COT = [pl.ds(0, 192), pl.ds(192, 64)]

    def send_cot(i):
        part = COT[i]
        return send(M_COTH + i, cot_h.at[part], cot.at[part, pl.ds(HALF, HALF)], head)

    s_coth = [send_cot(0)]

    for cp in ld_tok + ld_k + ld_v:
        cp.wait()

    def kv_tiles(b):
        def body(j, _):
            r = dot(tok[pl.ds(b * TOK, TOK), :], w[:, lanes(j, 256)]).astype(BF16)
            kv[pl.ds(b * TOK, TOK), lanes(j, 256)] = r
            return 0

        lax.fori_loop(0, 4, body, 0)

    kv_tiles(0)
    for cp in s_tok:
        cp.wait_recv()
    kv_tiles(1)

    for b in range(2):
        p0[pl.ds(b * 128, 128), :] = pool(kv[pl.ds(b * TOK, TOK), :])
    p1[...] = pool(p0[...])
    m_x1 = send(M_X1, p1, rows(S, (0, 128)), xhi)
    p2[...] = pool(p1[...])
    m_zo = [send(M_ZO, p2, rows(S, level_region(1, 0)), zdev[1])]
    p3[...] = pool(p2[...])
    m_zo += [send(M_ZO + k - 1, p3, rows(S, level_region(k, 0)), zdev[k]) for k in (2, 3)]
    p4[...] = pool(p3[...])
    m_y = [send(M_Y + k - 1, p4, ybuf.at[k - 1], ydev[k]) for k in (1, 2, 3)]

    for cp in ld_q:
        cp.wait()

    def q_body(j, _):
        qb[:, lanes(j, 256)] = dot(tok[...], w[:, pl.ds(pl.multiple_of(2 * WID + j * 256, 256), 256)]).astype(BF16)
        return 0

    lax.fori_loop(0, 2, q_body, 0)

    groups = [
        [(0, 256, 0.0), (256, 128, LN2)],
        [(384, 128, 2 * LN2)],
        [(512, 256, None)],
        [(768, 256, None)],
    ]
    chunks = [(gr, first, size) for gr in range(4) for first, size, _ in groups[gr]]
    r_iota = lax.broadcasted_iota(jnp.int32, (256, 256), 0)
    r_level = jnp.where(r_iota < 64, 3, jnp.where(r_iota < 128, 4, 5 + (r_iota // 16) % 2))
    ypb[...] = r_level.astype(F32) * LN2

    def source(first, size, b, h, value):
        col = pl.ds(pl.multiple_of(h * 128 + value * WID, 128), 128)
        if first == 0:
            return kv[pl.ds(b * TOK, TOK), col]
        if first == 256:
            return p0[pl.ds((1 - b) * 128, 128), col]
        return S[pl.ds(first - 384, size), col]

    def score(gr, h, b):
        it = h * 2 + b
        q = qb[pl.ds(b * TOK, TOK), lanes(h, 128)]
        parts = []
        peak = None
        for first, size, bias in groups[gr]:
            l = dot_t(source(first, size, b, h, 0), q) * SCALE
            if bias is None:
                l = l + ypb[...]
            elif bias:
                l = l + bias
            parts.append(l)
            top = jnp.max(l, axis=0, keepdims=True)
            peak = top if peak is None else jnp.maximum(peak, top)
        total = None
        for (first, size, _), l in zip(groups[gr], parts):
            e = jnp.exp(l - peak)
            E[it, pl.ds(first, size), :] = e
            part = jnp.sum(e, axis=0, keepdims=True)
            total = part if total is None else total + part
        stat[gr, it, 0:1, :] = peak
        stat[gr, it, 1:2, :] = total

    def grad_score(gr, h, b):
        it = h * 2 + b
        g = go[pl.ds(b * TOK, TOK), lanes(h, 128)]
        total = None
        for first, size, _ in groups[gr]:
            gp = dot_t(source(first, size, b, h, 1), g)
            GP[it, pl.ds(first, size), :] = gp
            part = jnp.sum(E[it, pl.ds(first, size), :] * gp, axis=0, keepdims=True)
            total = part if total is None else total + part
        stat[gr, it, 2:3, :] = total

    def each(*steps):
        def body(h, _):
            for b in range(2):
                for f, gr in steps:
                    f(gr, h, b)
            return 0

        lax.fori_loop(0, 4, body, 0)

    for cp in m_y:
        cp.wait_recv()
    wpl[pl.ds(0, 16), :] = ybuf[0]
    wpl[pl.ds(16, 16), :] = pool(jnp.concatenate([ybuf[1], ybuf[2]], axis=0))
    m_x2 = send(M_X2, wpl, rows(S, plane_region(0, 1)), xhi)
    s_coth.append(send_cot(1))
    m_zw = [send(M_ZW + k - 1, wpl, rows(S, plane_region(k, 0)), zdev[k]) for k in (1, 2, 3)]
    S[pl.ds(*plane_region(0, 0)), :] = wpl[...]

    each((score, 0))

    m_x1.wait_recv()
    p2x[...] = pool(S[pl.ds(0, 128), :])
    m_zx = [send(M_ZX, p2x, rows(S, level_region(1, 1)), zdev[1])]
    p3x[...] = pool(p2x[...])
    m_zx += [send(M_ZX + k - 1, p3x, rows(S, level_region(k, 1)), zdev[k]) for k in (2, 3)]
    each((score, 1))
    m_x2.wait_recv()
    m_zy = [
        send(M_ZY + k - 1, rows(S, plane_region(0, 1)), rows(S, plane_region(k, 1)), zdev[k])
        for k in (1, 2, 3)
    ]

    for cp in m_zo + m_zw:
        cp.wait_recv()
    each((score, 2))

    s_cotf = []
    for i in range(2):
        s_coth[i].wait_recv()
        s_cotf.append(send(
            M_COTF + i, cot.at[COT[i], pl.ds(HALF, HALF)],
            cot.at[pl.ds(TOK + 192 * i, (192, 64)[i]), pl.ds(HALF, HALF)], core,
        ))
    ld_cot.wait()
    for cp in ld_o:
        cp.wait()

    def go_tiles(b):
        def body(j, _):
            go[pl.ds(b * TOK, TOK), lanes(j, 256)] = dot_t(
                cot[pl.ds(b * TOK, TOK), :], wo[lanes(j, 256), :]
            ).astype(BF16)
            return 0

        lax.fori_loop(0, 2, body, 0)

    go_tiles(0)
    s_cotc.wait_recv()
    for cp in s_cotf:
        cp.wait_recv()
    go_tiles(1)

    each((grad_score, 0), (grad_score, 1), (grad_score, 2))

    for cp in m_zx + m_zy:
        cp.wait_recv()

    def finish(h, _):
        for b in range(2):
            it = h * 2 + b
            score(3, h, b)
            grad_score(3, h, b)
            peaks = [stat[gr, it, 0:1, :] for gr in range(4)]
            peak = jnp.maximum(jnp.maximum(peaks[0], peaks[1]), jnp.maximum(peaks[2], peaks[3]))
            scales = [jnp.exp(m - peak) for m in peaks]
            total = sum(f * stat[gr, it, 1:2, :] for gr, f in enumerate(scales))
            scales = [f / total for f in scales]
            for gr, f in enumerate(scales):
                fin[it, gr : gr + 1, :] = f
            fin[it, 4:5, :] = sum(f * stat[gr, it, 2:3, :] for gr, f in enumerate(scales))
            a = None
            for gr, first, size in chunks:
                pb = (E[it, pl.ds(first, size), :] * scales[gr]).astype(BF16)
                part = t_dot(source(first, size, b, h, 1), pb)
                a = part if a is None else a + part
            att[pl.ds(b * TOK, TOK), lanes(h, 128)] = a.T.astype(BF16)
        return 0

    lax.fori_loop(0, 4, finish, 0)

    def cols(i):
        return pl.ds(i * 512, 512)

    def out_piece(i):
        macc[:, cols(i)] = dot(att[pl.ds(0, TOK), :], wo[:, cols(i)])
        c_send[i] = dot(att[pl.ds(TOK, TOK), :], wo[:, cols(i)]).astype(BF16)
        return send(M_MIXC + i, c_send.at[i], c_recv.at[i], core)

    def head_piece(i, cp, total, got, base, src, dst):
        cp.wait_recv()
        src[i] = (total[pl.ds(0, TOK), cols(2 + i)] + got[2 + i].astype(F32)).astype(BF16)
        return send(base + i, src.at[i], dst.at[i], head)

    def last_piece(i, total, got, got_h):
        out_b[:, cols(i)] = (
            total[pl.ds(0, TOK), cols(i)] + got[i].astype(F32) + got_h[i].astype(F32)
        ).astype(BF16)

    s_mixc = {i: out_piece(i) for i in (2, 3, 0, 1)}
    s_mixh = [head_piece(i, s_mixc[2 + i], macc, c_recv, M_MIXH, h_send, h_recv) for i in (0, 1)]

    def backward(h, _):
        hcol = lanes(h, 128)
        vcol = pl.ds(pl.multiple_of(h * 128 + WID, 128), 128)
        for b in range(2):
            q = qb[pl.ds(b * TOK, TOK), hcol]
            g = go[pl.ds(b * TOK, TOK), hcol]
            it = h * 2 + b
            rd = fin[it, 4:5, :]
            dqt = None
            for gr, first, size in chunks:
                p = E[it, pl.ds(first, size), :] * fin[it, gr : gr + 1, :]
                dl = (p * (GP[it, pl.ds(first, size), :] - rd) * SCALE).astype(BF16)
                dvv = dot(p.astype(BF16), g)
                dkk = dot(dl, q)
                part = t_dot(source(first, size, b, h, 0), dl)
                dqt = part if dqt is None else dqt + part
                if first == 0:
                    dkv[pl.ds(b * TOK, TOK), hcol] = dkk
                    dkv[pl.ds(b * TOK, TOK), vcol] = dvv
                elif first == 256:
                    dp0[pl.ds((1 - b) * 128, 128), hcol] = dkk
                    dp0[pl.ds((1 - b) * 128, 128), vcol] = dvv
                elif b == 0:
                    dS[pl.ds(first - 384, size), hcol] = dkk
                    dS[pl.ds(first - 384, size), vcol] = dvv
                else:
                    dkk = dkk + dS[pl.ds(first - 384, size), hcol]
                    dvv = dvv + dS[pl.ds(first - 384, size), vcol]
                    dS[pl.ds(first - 384, size), hcol] = dkk
                    dS[pl.ds(first - 384, size), vcol] = dvv
                    sb[pl.ds(first - 384, size), hcol] = dkk.astype(BF16)
                    sb[pl.ds(first - 384, size), vcol] = dvv.astype(BF16)
            dq[pl.ds(b * TOK, TOK), hcol] = dqt.T.astype(BF16)
        return 0

    lax.fori_loop(0, 4, backward, 0)

    b_z, b_zy = {}, {}
    for dx in (1, 0):
        for k in (1, 2, 3):
            r = level_region(k, dx)
            b_z[k, dx] = send(B_Z + 2 * (k - 1) + dx, rows(sb, r), rows(RS, r), zdev[k])
            r = plane_region(k, dx)
            b_zy[k, dx] = send(B_ZY + 2 * (k - 1) + dx, rows(sb, r), rows(RS, r), zdev[k])

    for b in range(2):
        gk[pl.ds(b * TOK, TOK), :] = (
            spread(dp0[pl.ds(b * 128, 128), :]) + dkv[pl.ds(b * TOK, TOK), :]
        ).astype(BF16)

    def in_early(j, _):
        acc[:, lanes(j, 256)] = dot_t(dq[...], w[lanes(j, 256), pl.ds(2 * WID, WID)]) + dot_t(
            gk[...], w[lanes(j, 256), pl.ds(0, 2 * WID)]
        )
        return 0

    def collect(dx):
        for k in (1, 2, 3):
            b_z[k, dx].wait_recv()
            b_zy[k, dx].wait_recv()
        low = RS[pl.ds(*level_region(2, dx)), :].astype(F32) + RS[pl.ds(*level_region(3, dx)), :].astype(F32)
        top = spread(low) + RS[pl.ds(*level_region(1, dx)), :].astype(F32)
        plane = dS[pl.ds(*plane_region(0, dx)), :]
        for k in (1, 2, 3):
            plane = plane + RS[pl.ds(*plane_region(k, dx)), :].astype(F32)
        return top, plane

    lax.fori_loop(0, 8, in_early, 0)
    for i in range(4):
        s_mixc[i].wait_send()

    def in_piece(i):
        c_send[i] = acc[pl.ds(TOK, TOK), cols(i)].astype(BF16)
        return send(M_INC + i, c_send.at[i], ic_recv.at[i], core)

    s_inc = {i: in_piece(i) for i in (2, 3, 0, 1)}
    top, plane = collect(1)
    xa_s[pl.ds(0, 64), :] = top.astype(BF16)
    xa_s[pl.ds(64, 32), :] = plane.astype(BF16)
    b_xa = send(B_XA, xa_s, xa_r, xhi)
    s_inh = [head_piece(i, s_inc[2 + i], acc, ic_recv, M_INH, ih_send, ih_recv) for i in (0, 1)]
    b_x1 = send(B_X1, rows(sb, (0, 128)), rows(RS, (0, 128)), xhi)
    top, plane = collect(0)
    pf[pl.ds(0, 64), :] = top
    pf[pl.ds(64, 32), :] = plane

    b_xa.wait_recv()
    top = pf[pl.ds(0, 64), :] + xa_r[pl.ds(0, 64), :].astype(F32)
    plane = pf[pl.ds(64, 32), :] + xa_r[pl.ds(64, 32), :].astype(F32)
    gy_s[0] = plane[0:16].astype(BF16)
    high = spread(plane[16:32])
    gy_s[1] = high[0:16].astype(BF16)
    gy_s[2] = high[16:32].astype(BF16)
    b_y = [send(B_Y + k - 1, gy_s.at[k - 1], gy_r.at[k - 1], ydev[k]) for k in (1, 2, 3)]

    for i in (0, 1):
        s_mixc[i].wait_recv()
        s_mixh[i].wait_recv()
        last_piece(i, macc, c_recv, h_recv)
    st_mix = load(out_b, mix_o)

    for cp in b_y:
        cp.wait_recv()
    b_x1.wait_recv()
    g4 = gy_r[0].astype(F32) + gy_r[1].astype(F32) + gy_r[2].astype(F32)
    top = top + spread(spread(g4))
    low = spread(top) + RS[pl.ds(0, 128), :].astype(F32)
    low = low.astype(BF16)
    out_i = lax.broadcasted_iota(jnp.int32, (TOK, 64), 0)
    inp_i = lax.broadcasted_iota(jnp.int32, (TOK, 64), 1)
    quarter = jnp.where(out_i // 4 == inp_i, 0.25, 0.0).astype(BF16)

    def late_piece(i):
        late = dot_t(low, w[cols(i), pl.ds(0, 2 * WID)])
        lacc[:, cols(i)] = late[0:64]
        lc_send[i] = late[64:128].astype(BF16)
        return send(M_LC + i, lc_send.at[i], lc_recv.at[i], core)

    def late_head(i):
        s_lc[2 + i].wait_recv()
        lh_send[i] = (lacc[:, cols(2 + i)] + lc_recv[2 + i].astype(F32)).astype(BF16)
        return send(M_LH + i, lh_send.at[i], lh_recv.at[i], head)

    s_lc = {i: late_piece(i) for i in (2, 3)}
    s_lh = [late_head(0)]
    s_lc[0] = late_piece(0)
    s_lh.append(late_head(1))
    s_lc[1] = late_piece(1)
    st_mix.wait()
    for i in (0, 1):
        s_inc[i].wait_recv()
        s_inh[i].wait_recv()
        s_lc[i].wait_recv()
        s_lh[i].wait_recv()
        late = lacc[:, cols(i)] + lc_recv[i].astype(F32) + lh_recv[i].astype(F32)
        out_b[:, cols(i)] = (
            acc[pl.ds(0, TOK), cols(i)] + ic_recv[i].astype(F32) + ih_recv[i].astype(F32)
            + dot(quarter, late.astype(BF16))
        ).astype(BF16)
    st_in = load(out_b, ing_o)

    for i in (0, 1):
        s_mixh[i].wait_send()
    for cp in s_lh + list(s_lc.values()):
        cp.wait_send()
    for cp in s_tok + s_coth + s_cotf + s_inh + list(s_inc.values()) + [s_cotc, m_x1, m_x2, b_x1, b_xa]:
        cp.wait_send()
    for cp in m_y + m_zo + m_zw + m_zx + m_zy + b_y + list(b_z.values()) + list(b_zy.values()):
        cp.wait_send()
    st_in.wait()


def copy_out(a, b, a_o, b_o):
    a_o[...] = a[...]
    b_o[...] = b[...]


def per_device(tokens, w_query, w_key, w_value, w_out, cotangent):
    V = pltpu.VMEM
    scratch = [
        V((2 * TOK, 2 * HALF), BF16),
        V((2 * HALF, 3 * WID), BF16),
        V((WID, 2 * HALF), BF16),
        V((2 * TOK, 2 * HALF), BF16),
        V((2 * TOK, 2 * WID), BF16),
        V((2 * TOK, WID), BF16),
        V((2 * TOK, WID), BF16),
        V((256, 2 * WID), BF16),
        V((128, 2 * WID), BF16),
        V((64, 2 * WID), BF16),
        V((32, 2 * WID), BF16),
        V((16, 2 * WID), BF16),
        V((32, 2 * WID), BF16),
        V((64, 2 * WID), BF16),
        V((32, 2 * WID), BF16),
        V((3, 16, 2 * WID), BF16),
        V((ROWS, 2 * WID), BF16),
        V((96, 2 * WID), F32),
        V((8, 1024, 256), F32),
        V((4, 8, 8, 256), F32),
        V((8, 8, 256), F32),
        V((8, 1024, 256), F32),
        V((256, 256), F32),
        V((2 * TOK, WID), BF16),
        V((2 * TOK, 2 * HALF), F32),
        V((TOK, 2 * HALF), F32),
        V((4, TOK, 512), BF16),
        V((4, TOK, 512), BF16),
        V((2, TOK, 512), BF16),
        V((2, TOK, 512), BF16),
        V((4, TOK, 512), BF16),
        V((2, TOK, 512), BF16),
        V((2, TOK, 512), BF16),
        V((64, 2 * HALF), F32),
        V((4, 64, 512), BF16),
        V((4, 64, 512), BF16),
        V((2, 64, 512), BF16),
        V((2, 64, 512), BF16),
        V((2 * TOK, 2 * WID), F32),
        V((256, 2 * WID), F32),
        V((ROWS, 2 * WID), F32),
        V((ROWS, 2 * WID), BF16),
        V((ROWS, 2 * WID), BF16),
        V((96, 2 * WID), BF16),
        V((96, 2 * WID), BF16),
        V((3, 16, 2 * WID), BF16),
        V((3, 16, 2 * WID), BF16),
        V((2 * TOK, WID), BF16),
        V((2 * TOK, 2 * WID), BF16),
        V((TOK, HALF), BF16),
        pltpu.SemaphoreType.DMA((16,)),
        pltpu.SemaphoreType.DMA((N_MSG,)),
        pltpu.SemaphoreType.DMA((N_MSG,)),
    ]
    any_spec = pl.BlockSpec(memory_space=pl.ANY)
    out = jax.ShapeDtypeStruct((TOK, HALF), BF16)
    mixed, input_grad = pl.pallas_call(
        kernel,
        out_shape=(out, out),
        in_specs=[any_spec] * 6,
        out_specs=(any_spec, any_spec),
        scratch_shapes=scratch,
        compiler_params=pltpu.CompilerParams(
            collective_id=0, has_side_effects=True, vmem_limit_bytes=60 * 2**20
        ),
    )(tokens, w_query, w_key, w_value, w_out, cotangent)
    return pl.pallas_call(
        copy_out,
        grid=(2,),
        out_shape=(out, out),
        in_specs=[pl.BlockSpec((TOK // 2, HALF), lambda i: (i, 0))] * 2,
        out_specs=[pl.BlockSpec((TOK // 2, HALF), lambda i: (i, 0))] * 2,
    )(mixed, input_grad)


def solution(mesh):
    return jax.shard_map(
        per_device,
        mesh=mesh,
        in_specs=(
            P("seq", None), P(None, "head"), P(None, "head"), P(None, "head"),
            P("head", None), P("seq", "head"),
        ),
        out_specs=(P("seq", "head"), P("seq", "head")),
        check_vma=False,
    )
```

time: 103 us -> 87 us (0.84)
  Pallas kernels: 98.1 us -> 86.2 us
  local copies, waits for them, and re-layouts: 3.74 us -> 0 us
    pallas_call x1, Pallas kernels: 98.1 us -> 84.2 us  [per_device(): pl.pallas_call(kernel, out_shape=(out, out), in_specs=[any_spec] * 6, out...]
    unnamed x2 -> x0, local copies, waits for them, and re-layouts: 3.74 us -> none
    pallas_call x0 -> x1, Pallas kernels: none -> 2.04 us  [per_device(): pl.pallas_call(copy_out, grid=(2,), out_shape=(out, out), in_specs=[pl.Bl...]
where the time goes in v1:
time: 87 us; the launch traced here: 86.8 us
  Pallas kernels  86.2 us (99%)
    pallas_call x1, Pallas kernels, per_device(): pl.pallas_call(kernel, out_shape=(out, out), in_specs=[any_spec] * 6, out...  84.2 us
    pallas_call x1, Pallas kernels, per_device(): pl.pallas_call(copy_out, grid=(2,), out_shape=(out, out), in_specs=[pl.Bl...  2.04 us

profile of v1, /device:TPU:1, one launch (start us, length us, event | category | flops | bytes accessed | tf_op | source)
XLA Modules:
  0.0 86.8 jit_solution(5524560544910441770)
XLA Ops:
  0.6 84.2 %shard_map.77 = (bf16[256,1024]{1,0:T(8,128)(2,1)}, bf16[256,1024]{1,0:T(8,128)(2,1)}) custom-call(bf16[256,2048]{1,0:T(8,128)(2,1)} %tok_h.1, bf16[2048,1024]{1,0:T(8,128)(2,1)} %wq_h.1, bf16[2048,1024]{1,0:T(8,128)(2,1)} %wk_h.1, bf16[2048,1024]{1,0:T(8,128)(2,1)} %wv_h.1, bf16[1024,2048]{1,0:T(8,128)(2,1)} %wo_h.1, bf16[256,1024]{1,0:T(8,128)(2,1)} %cot_h.1), custom_call_target="tpu_custom_call" | custom-call | tf_op jit(solution)/shard_map/pallas_call | solution.py:554
  84.8 2.0 %shard_map.78 = (bf16[256,1024]{1,0:T(8,128)(2,1)}, bf16[256,1024]{1,0:T(8,128)(2,1)}) custom-call(bf16[256,1024]{1,0:T(8,128)(2,1)} %get-tuple-element.4.a, bf16[256,1024]{1,0:T(8,128)(2,1)} %get-tuple-element.5.b), custom_call_target="tpu_custom_call" | custom-call | tf_op jit(solution)/shard_map/pallas_call | solution.py:564

commit v2 on v1

--- a/solution.py
+++ b/solution.py
@@ -1,3 +1,4 @@
+import functools
 import math
 
 import jax
@@ -60,8 +61,8 @@
 (
     M_TOK, M_COTC, M_COTH, M_COTF, M_MIXC, M_MIXH, M_INC, M_INH,
     M_Y, M_X1, M_X2, M_ZO, M_ZW, M_ZX, M_ZY,
-    B_X1, B_XA, B_Z, B_ZY, B_Y, M_LC, M_LH, N_MSG,
-) = (0, 2, 3, 5, 7, 11, 13, 17, 19, 22, 23, 24, 27, 30, 33, 36, 37, 38, 44, 50, 53, 57, 59)
+    B_XA, B_Z, B_ZY, B_Y, M_LC, M_LH, N_MSG,
+) = (0, 2, 3, 5, 7, 11, 13, 17, 19, 22, 23, 24, 27, 30, 33, 36, 37, 49, 61, 64, 68, 70)
 
 
 def kernel(
@@ -125,8 +126,6 @@
         send(M_TOK + i, tok_h.at[:, a], tok.at[pl.ds(TOK, TOK), b], core)
         for i, (a, b) in enumerate(halves)
     ]
-    s_cotc = send(M_COTC, cot_h, cot.at[pl.ds(TOK, TOK), pl.ds(0, HALF)], core)
-
     COT = [pl.ds(0, 192), pl.ds(192, 64)]
 
     def send_cot(i):
@@ -149,6 +148,7 @@
     kv_tiles(0)
     for cp in s_tok:
         cp.wait_recv()
+    s_cotc = send(M_COTC, cot_h, cot.at[pl.ds(TOK, TOK), pl.ds(0, HALF)], core)
     kv_tiles(1)
 
     for b in range(2):
@@ -175,9 +175,10 @@
         [(0, 256, 0.0), (256, 128, LN2)],
         [(384, 128, 2 * LN2)],
         [(512, 256, None)],
-        [(768, 256, None)],
+        [(768, 128, None)],
+        [(896, 128, None)],
     ]
-    chunks = [(gr, first, size) for gr in range(4) for first, size, _ in groups[gr]]
+    chunks = [(gr, first, size) for gr in range(5) for first, size, _ in groups[gr]]
     r_iota = lax.broadcasted_iota(jnp.int32, (256, 256), 0)
     r_level = jnp.where(r_iota < 64, 3, jnp.where(r_iota < 128, 4, 5 + (r_iota // 16) % 2))
     ypb[...] = r_level.astype(F32) * LN2
@@ -198,7 +199,7 @@
         for first, size, bias in groups[gr]:
             l = dot_t(source(first, size, b, h, 0), q) * SCALE
             if bias is None:
-                l = l + ypb[...]
+                l = l + ypb[pl.ds((first - 512) % 256, size), :]
             elif bias:
                 l = l + bias
             parts.append(l)
@@ -238,7 +239,6 @@
     wpl[pl.ds(0, 16), :] = ybuf[0]
     wpl[pl.ds(16, 16), :] = pool(jnp.concatenate([ybuf[1], ybuf[2]], axis=0))
     m_x2 = send(M_X2, wpl, rows(S, plane_region(0, 1)), xhi)
-    s_coth.append(send_cot(1))
     m_zw = [send(M_ZW + k - 1, wpl, rows(S, plane_region(k, 0)), zdev[k]) for k in (1, 2, 3)]
     S[pl.ds(*plane_region(0, 0)), :] = wpl[...]
 
@@ -251,6 +251,7 @@
     m_zx += [send(M_ZX + k - 1, p3x, rows(S, level_region(k, 1)), zdev[k]) for k in (2, 3)]
     each((score, 1))
     m_x2.wait_recv()
+    s_coth.append(send_cot(1))
     m_zy = [
         send(M_ZY + k - 1, rows(S, plane_region(0, 1)), rows(S, plane_region(k, 1)), zdev[k])
         for k in (1, 2, 3)
@@ -288,22 +289,25 @@
 
     each((grad_score, 0), (grad_score, 1), (grad_score, 2))
 
-    for cp in m_zx + m_zy:
+    for cp in m_zx:
+        cp.wait_recv()
+    each((score, 3), (grad_score, 3))
+    for cp in m_zy:
         cp.wait_recv()
 
     def finish(h, _):
         for b in range(2):
             it = h * 2 + b
-            score(3, h, b)
-            grad_score(3, h, b)
-            peaks = [stat[gr, it, 0:1, :] for gr in range(4)]
-            peak = jnp.maximum(jnp.maximum(peaks[0], peaks[1]), jnp.maximum(peaks[2], peaks[3]))
+            score(4, h, b)
+            grad_score(4, h, b)
+            peaks = [stat[gr, it, 0:1, :] for gr in range(5)]
+            peak = functools.reduce(jnp.maximum, peaks)
             scales = [jnp.exp(m - peak) for m in peaks]
             total = sum(f * stat[gr, it, 1:2, :] for gr, f in enumerate(scales))
             scales = [f / total for f in scales]
             for gr, f in enumerate(scales):
                 fin[it, gr : gr + 1, :] = f
-            fin[it, 4:5, :] = sum(f * stat[gr, it, 2:3, :] for gr, f in enumerate(scales))
+            fin[it, 5:6, :] = sum(f * stat[gr, it, 2:3, :] for gr, f in enumerate(scales))
             a = None
             for gr, first, size in chunks:
                 pb = (E[it, pl.ds(first, size), :] * scales[gr]).astype(BF16)
@@ -335,14 +339,15 @@
     s_mixc = {i: out_piece(i) for i in (2, 3, 0, 1)}
     s_mixh = [head_piece(i, s_mixc[2 + i], macc, c_recv, M_MIXH, h_send, h_recv) for i in (0, 1)]
 
-    def backward(h, _):
+    def backward(pair, i):
+        h = 2 * pair + i
         hcol = lanes(h, 128)
         vcol = pl.ds(pl.multiple_of(h * 128 + WID, 128), 128)
         for b in range(2):
             q = qb[pl.ds(b * TOK, TOK), hcol]
             g = go[pl.ds(b * TOK, TOK), hcol]
             it = h * 2 + b
-            rd = fin[it, 4:5, :]
+            rd = fin[it, 5:6, :]
             dqt = None
             for gr, first, size in chunks:
                 p = E[it, pl.ds(first, size), :] * fin[it, gr : gr + 1, :]
@@ -365,20 +370,32 @@
                     dvv = dvv + dS[pl.ds(first - 384, size), vcol]
                     dS[pl.ds(first - 384, size), hcol] = dkk
                     dS[pl.ds(first - 384, size), vcol] = dvv
-                    sb[pl.ds(first - 384, size), hcol] = dkk.astype(BF16)
-                    sb[pl.ds(first - 384, size), vcol] = dvv.astype(BF16)
+                    if first > 384:
+                        sb[pair, pl.ds(first - 384, size), lanes(i, 128)] = dkk.astype(BF16)
+                        sb[pair, pl.ds(first - 384, size), lanes(i + 2, 128)] = dvv.astype(BF16)
             dq[pl.ds(b * TOK, TOK), hcol] = dqt.T.astype(BF16)
-        return 0
-
-    lax.fori_loop(0, 4, backward, 0)
-
-    b_z, b_zy = {}, {}
-    for dx in (1, 0):
+
+    def heads(pair):
+        def body(i, _):
+            backward(pair, i)
+            return 0
+
+        lax.fori_loop(0, 2, body, 0)
+
+    b_z = {0: [], 1: []}
+
+    def send_z(pair, dx):
         for k in (1, 2, 3):
-            r = level_region(k, dx)
-            b_z[k, dx] = send(B_Z + 2 * (k - 1) + dx, rows(sb, r), rows(RS, r), zdev[k])
-            r = plane_region(k, dx)
-            b_zy[k, dx] = send(B_ZY + 2 * (k - 1) + dx, rows(sb, r), rows(RS, r), zdev[k])
+            for base, r in ((B_Z, level_region(k, dx)), (B_ZY, plane_region(k, dx))):
+                n = base + 4 * (k - 1) + 2 * dx + pair
+                b_z[dx].append(send(n, rows(sb.at[pair], r), rows(RS.at[pair], r), zdev[k]))
+
+    heads(0)
+    send_z(0, 1)
+    heads(1)
+    send_z(1, 1)
+    send_z(0, 0)
+    send_z(1, 0)
 
     for b in range(2):
         gk[pl.ds(b * TOK, TOK), :] = (
@@ -391,15 +408,18 @@
         )
         return 0
 
+    def returned(region):
+        a, b = RS[0, pl.ds(*region), :], RS[1, pl.ds(*region), :]
+        return jnp.concatenate([a[:, :256], b[:, :256], a[:, 256:], b[:, 256:]], axis=1).astype(F32)
+
     def collect(dx):
-        for k in (1, 2, 3):
-            b_z[k, dx].wait_recv()
-            b_zy[k, dx].wait_recv()
-        low = RS[pl.ds(*level_region(2, dx)), :].astype(F32) + RS[pl.ds(*level_region(3, dx)), :].astype(F32)
-        top = spread(low) + RS[pl.ds(*level_region(1, dx)), :].astype(F32)
+        for cp in b_z[dx]:
+            cp.wait_recv()
+        low = returned(level_region(2, dx)) + returned(level_region(3, dx))
+        top = spread(low) + returned(level_region(1, dx))
         plane = dS[pl.ds(*plane_region(0, dx)), :]
         for k in (1, 2, 3):
-            plane = plane + RS[pl.ds(*plane_region(k, dx)), :].astype(F32)
+            plane = plane + returned(plane_region(k, dx))
         return top, plane
 
     lax.fori_loop(0, 8, in_early, 0)
@@ -412,18 +432,17 @@
 
     s_inc = {i: in_piece(i) for i in (2, 3, 0, 1)}
     top, plane = collect(1)
-    xa_s[pl.ds(0, 64), :] = top.astype(BF16)
-    xa_s[pl.ds(64, 32), :] = plane.astype(BF16)
+    xa_s[pl.ds(0, 128), :] = (spread(top) + dS[pl.ds(0, 128), :]).astype(BF16)
+    xa_s[pl.ds(128, 32), :] = plane.astype(BF16)
     b_xa = send(B_XA, xa_s, xa_r, xhi)
     s_inh = [head_piece(i, s_inc[2 + i], acc, ic_recv, M_INH, ih_send, ih_recv) for i in (0, 1)]
-    b_x1 = send(B_X1, rows(sb, (0, 128)), rows(RS, (0, 128)), xhi)
     top, plane = collect(0)
     pf[pl.ds(0, 64), :] = top
     pf[pl.ds(64, 32), :] = plane
 
     b_xa.wait_recv()
-    top = pf[pl.ds(0, 64), :] + xa_r[pl.ds(0, 64), :].astype(F32)
-    plane = pf[pl.ds(64, 32), :] + xa_r[pl.ds(64, 32), :].astype(F32)
+    top = pf[pl.ds(0, 64), :]
+    plane = pf[pl.ds(64, 32), :] + xa_r[pl.ds(128, 32), :].astype(F32)
     gy_s[0] = plane[0:16].astype(BF16)
     high = spread(plane[16:32])
     gy_s[1] = high[0:16].astype(BF16)
@@ -438,10 +457,9 @@
 
     for cp in b_y:
         cp.wait_recv()
-    b_x1.wait_recv()
     g4 = gy_r[0].astype(F32) + gy_r[1].astype(F32) + gy_r[2].astype(F32)
     top = top + spread(spread(g4))
-    low = spread(top) + RS[pl.ds(0, 128), :].astype(F32)
+    low = spread(top) + xa_r[pl.ds(0, 128), :].astype(F32)
     low = low.astype(BF16)
     out_i = lax.broadcasted_iota(jnp.int32, (TOK, 64), 0)
     inp_i = lax.broadcasted_iota(jnp.int32, (TOK, 64), 1)
@@ -480,9 +498,9 @@
         s_mixh[i].wait_send()
     for cp in s_lh + list(s_lc.values()):
         cp.wait_send()
-    for cp in s_tok + s_coth + s_cotf + s_inh + list(s_inc.values()) + [s_cotc, m_x1, m_x2, b_x1, b_xa]:
+    for cp in s_tok + s_coth + s_cotf + s_inh + list(s_inc.values()) + [s_cotc, m_x1, m_x2, b_xa]:
         cp.wait_send()
-    for cp in m_y + m_zo + m_zw + m_zx + m_zy + b_y + list(b_z.values()) + list(b_zy.values()):
+    for cp in m_y + m_zo + m_zw + m_zx + m_zy + b_y + b_z[0] + b_z[1]:
         cp.wait_send()
     st_in.wait()
 
@@ -514,7 +532,7 @@
         V((ROWS, 2 * WID), BF16),
         V((96, 2 * WID), F32),
         V((8, 1024, 256), F32),
-        V((4, 8, 8, 256), F32),
+        V((5, 8, 8, 256), F32),
         V((8, 8, 256), F32),
         V((8, 1024, 256), F32),
         V((256, 256), F32),
@@ -536,10 +554,10 @@
         V((2 * TOK, 2 * WID), F32),
         V((256, 2 * WID), F32),
         V((ROWS, 2 * WID), F32),
-        V((ROWS, 2 * WID), BF16),
-        V((ROWS, 2 * WID), BF16),
-        V((96, 2 * WID), BF16),
-        V((96, 2 * WID), BF16),
+        V((2, ROWS, WID), BF16),
+        V((2, ROWS, WID), BF16),
+        V((160, 2 * WID), BF16),
+        V((160, 2 * WID), BF16),
         V((3, 16, 2 * WID), BF16),
         V((3, 16, 2 * WID), BF16),
         V((2 * TOK, WID), BF16),

time: 87 us -> 79.9 us (0.918)
  Pallas kernels: 86.2 us -> 78.8 us
    pallas_call x1, Pallas kernels: 84.2 us -> 76.7 us  [per_device(): pl.pallas_call(kernel, out_shape=(out, out), in_specs=[any_spec] * 6, out...]
where the time goes in v2:
time: 79.9 us; the launch traced here: 79.4 us
  Pallas kernels  78.8 us (99%)
    pallas_call x1, Pallas kernels, per_device(): pl.pallas_call(kernel, out_shape=(out, out), in_specs=[any_spec] * 6, out...  76.7 us
    pallas_call x1, Pallas kernels, per_device(): pl.pallas_call(copy_out, grid=(2,), out_shape=(out, out), in_specs=[pl.Bl...  2.04 us

profile of v2, /device:TPU:1, one launch (start us, length us, event | category | flops | bytes accessed | tf_op | source)
XLA Modules:
  0.0 79.4 jit_solution(16428838716529442311)
XLA Ops:
  0.6 76.7 %shard_map.77 = (bf16[256,1024]{1,0:T(8,128)(2,1)}, bf16[256,1024]{1,0:T(8,128)(2,1)}) custom-call(bf16[256,2048]{1,0:T(8,128)(2,1)} %tok_h.1, bf16[2048,1024]{1,0:T(8,128)(2,1)} %wq_h.1, bf16[2048,1024]{1,0:T(8,128)(2,1)} %wk_h.1, bf16[2048,1024]{1,0:T(8,128)(2,1)} %wv_h.1, bf16[1024,2048]{1,0:T(8,128)(2,1)} %wo_h.1, bf16[256,1024]{1,0:T(8,128)(2,1)} %cot_h.1), custom_call_target="tpu_custom_call" | custom-call | tf_op jit(solution)/shard_map/pallas_call | solution.py:572
  77.4 2.0 %shard_map.78 = (bf16[256,1024]{1,0:T(8,128)(2,1)}, bf16[256,1024]{1,0:T(8,128)(2,1)}) custom-call(bf16[256,1024]{1,0:T(8,128)(2,1)} %get-tuple-element.4.a, bf16[256,1024]{1,0:T(8,128)(2,1)} %get-tuple-element.5.b), custom_call_target="tpu_custom_call" | custom-call | tf_op jit(solution)/shard_map/pallas_call | solution.py:582

commit v3 on v2

--- a/solution.py
+++ b/solution.py
@@ -24,6 +24,10 @@
     return (128 + dx * 256, 64) if dz == 1 else (128 + dx * 256 + 32 * dz, 32)
 
 
+def half(region, b):
+    return (region[0] + b * region[1] // 2, region[1] // 2)
+
+
 def plane_region(dz, dx):
     return (256 + dx * 256 + 32 * dz, 32)
 
@@ -62,7 +66,7 @@
     M_TOK, M_COTC, M_COTH, M_COTF, M_MIXC, M_MIXH, M_INC, M_INH,
     M_Y, M_X1, M_X2, M_ZO, M_ZW, M_ZX, M_ZY,
     B_XA, B_Z, B_ZY, B_Y, M_LC, M_LH, N_MSG,
-) = (0, 2, 3, 5, 7, 11, 13, 17, 19, 22, 23, 24, 27, 30, 33, 36, 37, 49, 61, 64, 68, 70)
+) = (0, 2, 3, 5, 7, 11, 13, 17, 19, 22, 24, 25, 31, 34, 40, 43, 44, 56, 68, 71, 75, 77)
 
 
 def kernel(
@@ -101,9 +105,6 @@
     ld_tok = [load(tok_h.at[:, a], tok.at[pl.ds(0, TOK), b]) for a, b in halves]
     ld_k = [load(wk_h.at[a, wcol], w.at[b, pl.ds(0, WID)]) for a, b in halves]
     ld_v = [load(wv_h.at[a, wcol], w.at[b, pl.ds(WID, WID)]) for a, b in halves]
-    ld_q = [load(wq_h.at[a, wcol], w.at[b, pl.ds(2 * WID, WID)]) for a, b in halves]
-    ld_cot = load(cot_h, cot.at[pl.ds(0, TOK), pl.ds(0, HALF)])
-    ld_o = [load(wo_h.at[wcol, a], wo.at[:, b]) for a, b in halves]
 
     barrier = pltpu.get_barrier_semaphore()
     partners = [core, head, xhi] + [zdev[k] for k in (1, 2, 3)] + [ydev[k] for k in (1, 2, 3)]
@@ -126,7 +127,7 @@
         send(M_TOK + i, tok_h.at[:, a], tok.at[pl.ds(TOK, TOK), b], core)
         for i, (a, b) in enumerate(halves)
     ]
-    COT = [pl.ds(0, 192), pl.ds(192, 64)]
+    COT = [pl.ds(0, 96), pl.ds(96, 160)]
 
     def send_cot(i):
         part = COT[i]
@@ -136,6 +137,9 @@
 
     for cp in ld_tok + ld_k + ld_v:
         cp.wait()
+    ld_q = [load(wq_h.at[a, wcol], w.at[b, pl.ds(2 * WID, WID)]) for a, b in halves]
+    ld_cot = load(cot_h, cot.at[pl.ds(0, TOK), pl.ds(0, HALF)])
+    ld_o = [load(wo_h.at[wcol, a], wo.at[:, b]) for a, b in halves]
 
     def kv_tiles(b):
         def body(j, _):
@@ -145,20 +149,30 @@
 
         lax.fori_loop(0, 4, body, 0)
 
+    m_x1, m_zo, m_zx = [], [], []
+
+    def pool_block(b):
+        p0[pl.ds(b * 128, 128), :] = pool(kv[pl.ds(b * TOK, TOK), :])
+        p1[pl.ds(b * 64, 64), :] = pool(p0[pl.ds(b * 128, 128), :])
+        m_x1.append(send(M_X1 + b, rows(p1, (b * 64, 64)), rows(S, (b * 64, 64)), xhi))
+        p2[pl.ds(b * 32, 32), :] = pool(p1[pl.ds(b * 64, 64), :])
+        p3[pl.ds(b * 16, 16), :] = pool(p2[pl.ds(b * 32, 32), :])
+        m_zo.extend(pass_z(M_ZO, b, 0, p2, p3))
+
+    def pass_z(base, b, dx, two, three):
+        out = []
+        for k in (1, 2, 3):
+            src = rows(two, (b * 32, 32)) if k == 1 else rows(three, (b * 16, 16))
+            out.append(send(base + 2 * (k - 1) + b, src, rows(S, half(level_region(k, dx), b)), zdev[k]))
+        return out
+
     kv_tiles(0)
+    pool_block(0)
     for cp in s_tok:
         cp.wait_recv()
     s_cotc = send(M_COTC, cot_h, cot.at[pl.ds(TOK, TOK), pl.ds(0, HALF)], core)
     kv_tiles(1)
-
-    for b in range(2):
-        p0[pl.ds(b * 128, 128), :] = pool(kv[pl.ds(b * TOK, TOK), :])
-    p1[...] = pool(p0[...])
-    m_x1 = send(M_X1, p1, rows(S, (0, 128)), xhi)
-    p2[...] = pool(p1[...])
-    m_zo = [send(M_ZO, p2, rows(S, level_region(1, 0)), zdev[1])]
-    p3[...] = pool(p2[...])
-    m_zo += [send(M_ZO + k - 1, p3, rows(S, level_region(k, 0)), zdev[k]) for k in (2, 3)]
+    pool_block(1)
     p4[...] = pool(p3[...])
     m_y = [send(M_Y + k - 1, p4, ybuf.at[k - 1], ydev[k]) for k in (1, 2, 3)]
 
@@ -214,17 +228,6 @@
         stat[gr, it, 0:1, :] = peak
         stat[gr, it, 1:2, :] = total
 
-    def grad_score(gr, h, b):
-        it = h * 2 + b
-        g = go[pl.ds(b * TOK, TOK), lanes(h, 128)]
-        total = None
-        for first, size, _ in groups[gr]:
-            gp = dot_t(source(first, size, b, h, 1), g)
-            GP[it, pl.ds(first, size), :] = gp
-            part = jnp.sum(E[it, pl.ds(first, size), :] * gp, axis=0, keepdims=True)
-            total = part if total is None else total + part
-        stat[gr, it, 2:3, :] = total
-
     def each(*steps):
         def body(h, _):
             for b in range(2):
@@ -242,13 +245,15 @@
     m_zw = [send(M_ZW + k - 1, wpl, rows(S, plane_region(k, 0)), zdev[k]) for k in (1, 2, 3)]
     S[pl.ds(*plane_region(0, 0)), :] = wpl[...]
 
+    def pass_x(b):
+        m_x1[b].wait_recv()
+        p2x[pl.ds(b * 32, 32), :] = pool(S[pl.ds(b * 64, 64), :])
+        p3x[pl.ds(b * 16, 16), :] = pool(p2x[pl.ds(b * 32, 32), :])
+        m_zx.extend(pass_z(M_ZX, b, 1, p2x, p3x))
+
+    pass_x(0)
     each((score, 0))
-
-    m_x1.wait_recv()
-    p2x[...] = pool(S[pl.ds(0, 128), :])
-    m_zx = [send(M_ZX, p2x, rows(S, level_region(1, 1)), zdev[1])]
-    p3x[...] = pool(p2x[...])
-    m_zx += [send(M_ZX + k - 1, p3x, rows(S, level_region(k, 1)), zdev[k]) for k in (2, 3)]
+    pass_x(1)
     each((score, 1))
     m_x2.wait_recv()
     s_coth.append(send_cot(1))
@@ -261,45 +266,19 @@
         cp.wait_recv()
     each((score, 2))
 
-    s_cotf = []
-    for i in range(2):
-        s_coth[i].wait_recv()
-        s_cotf.append(send(
-            M_COTF + i, cot.at[COT[i], pl.ds(HALF, HALF)],
-            cot.at[pl.ds(TOK + 192 * i, (192, 64)[i]), pl.ds(HALF, HALF)], core,
-        ))
-    ld_cot.wait()
+    for cp in m_zx:
+        cp.wait_recv()
+    each((score, 3))
+    for cp in m_zy:
+        cp.wait_recv()
+
     for cp in ld_o:
         cp.wait()
-
-    def go_tiles(b):
-        def body(j, _):
-            go[pl.ds(b * TOK, TOK), lanes(j, 256)] = dot_t(
-                cot[pl.ds(b * TOK, TOK), :], wo[lanes(j, 256), :]
-            ).astype(BF16)
-            return 0
-
-        lax.fori_loop(0, 2, body, 0)
-
-    go_tiles(0)
-    s_cotc.wait_recv()
-    for cp in s_cotf:
-        cp.wait_recv()
-    go_tiles(1)
-
-    each((grad_score, 0), (grad_score, 1), (grad_score, 2))
-
-    for cp in m_zx:
-        cp.wait_recv()
-    each((score, 3), (grad_score, 3))
-    for cp in m_zy:
-        cp.wait_recv()
 
     def finish(h, _):
         for b in range(2):
             it = h * 2 + b
             score(4, h, b)
-            grad_score(4, h, b)
             peaks = [stat[gr, it, 0:1, :] for gr in range(5)]
             peak = functools.reduce(jnp.maximum, peaks)
             scales = [jnp.exp(m - peak) for m in peaks]
@@ -307,7 +286,6 @@
             scales = [f / total for f in scales]
             for gr, f in enumerate(scales):
                 fin[it, gr : gr + 1, :] = f
-            fin[it, 5:6, :] = sum(f * stat[gr, it, 2:3, :] for gr, f in enumerate(scales))
             a = None
             for gr, first, size in chunks:
                 pb = (E[it, pl.ds(first, size), :] * scales[gr]).astype(BF16)
@@ -338,6 +316,30 @@
 
     s_mixc = {i: out_piece(i) for i in (2, 3, 0, 1)}
     s_mixh = [head_piece(i, s_mixc[2 + i], macc, c_recv, M_MIXH, h_send, h_recv) for i in (0, 1)]
+
+    s_cotf = []
+    for i in range(2):
+        s_coth[i].wait_recv()
+        s_cotf.append(send(
+            M_COTF + i, cot.at[COT[i], pl.ds(HALF, HALF)],
+            cot.at[pl.ds(TOK + 96 * i, (96, 160)[i]), pl.ds(HALF, HALF)], core,
+        ))
+    ld_cot.wait()
+
+    def go_tiles(b):
+        def body(j, _):
+            go[pl.ds(b * TOK, TOK), lanes(j, 256)] = dot_t(
+                cot[pl.ds(b * TOK, TOK), :], wo[lanes(j, 256), :]
+            ).astype(BF16)
+            return 0
+
+        lax.fori_loop(0, 2, body, 0)
+
+    go_tiles(0)
+    s_cotc.wait_recv()
+    for cp in s_cotf:
+        cp.wait_recv()
+    go_tiles(1)
 
     def backward(pair, i):
         h = 2 * pair + i
@@ -347,11 +349,18 @@
             q = qb[pl.ds(b * TOK, TOK), hcol]
             g = go[pl.ds(b * TOK, TOK), hcol]
             it = h * 2 + b
-            rd = fin[it, 5:6, :]
+            scales = [fin[it, gr : gr + 1, :] for gr in range(5)]
+            rd = None
+            for gr, first, size in chunks:
+                gp = dot_t(source(first, size, b, h, 1), g)
+                GP[pl.ds(first, size), :] = gp
+                p = E[it, pl.ds(first, size), :] * scales[gr]
+                part = jnp.sum(p * gp, axis=0, keepdims=True)
+                rd = part if rd is None else rd + part
             dqt = None
             for gr, first, size in chunks:
-                p = E[it, pl.ds(first, size), :] * fin[it, gr : gr + 1, :]
-                dl = (p * (GP[it, pl.ds(first, size), :] - rd) * SCALE).astype(BF16)
+                p = E[it, pl.ds(first, size), :] * scales[gr]
+                dl = (p * (GP[pl.ds(first, size), :] - rd) * SCALE).astype(BF16)
                 dvv = dot(p.astype(BF16), g)
                 dkk = dot(dl, q)
                 part = t_dot(source(first, size, b, h, 0), dl)
@@ -498,9 +507,9 @@
         s_mixh[i].wait_send()
     for cp in s_lh + list(s_lc.values()):
         cp.wait_send()
-    for cp in s_tok + s_coth + s_cotf + s_inh + list(s_inc.values()) + [s_cotc, m_x1, m_x2, b_xa]:
+    for cp in s_tok + s_coth + s_cotf + s_inh + list(s_inc.values()) + [s_cotc, m_x2, b_xa]:
         cp.wait_send()
-    for cp in m_y + m_zo + m_zw + m_zx + m_zy + b_y + b_z[0] + b_z[1]:
+    for cp in m_x1 + m_y + m_zo + m_zw + m_zx + m_zy + b_y + b_z[0] + b_z[1]:
         cp.wait_send()
     st_in.wait()
 
@@ -534,7 +543,7 @@
         V((8, 1024, 256), F32),
         V((5, 8, 8, 256), F32),
         V((8, 8, 256), F32),
-        V((8, 1024, 256), F32),
+        V((1024, 256), F32),
         V((256, 256), F32),
         V((2 * TOK, WID), BF16),
         V((2 * TOK, 2 * HALF), F32),

time: 79.9 us -> 77.1 us (0.965)
  Pallas kernels: 78.8 us -> 76.2 us
    pallas_call x1, Pallas kernels: 76.7 us -> 74.1 us  [per_device(): pl.pallas_call(kernel, out_shape=(out, out), in_specs=[any_spec] * 6, out...]
where the time goes in v3:
time: 77.1 us; the launch traced here: 76.8 us
  Pallas kernels  76.2 us (99%)
    pallas_call x1, Pallas kernels, per_device(): pl.pallas_call(kernel, out_shape=(out, out), in_specs=[any_spec] * 6, out...  74.1 us
    pallas_call x1, Pallas kernels, per_device(): pl.pallas_call(copy_out, grid=(2,), out_shape=(out, out), in_specs=[pl.Bl...  2.04 us

profile of v3, /device:TPU:1, one launch (start us, length us, event | category | flops | bytes accessed | tf_op | source)
XLA Modules:
  0.0 76.8 jit_solution(12090059162721172313)
XLA Ops:
  0.6 74.1 %shard_map.77 = (bf16[256,1024]{1,0:T(8,128)(2,1)}, bf16[256,1024]{1,0:T(8,128)(2,1)}) custom-call(bf16[256,2048]{1,0:T(8,128)(2,1)} %tok_h.1, bf16[2048,1024]{1,0:T(8,128)(2,1)} %wq_h.1, bf16[2048,1024]{1,0:T(8,128)(2,1)} %wk_h.1, bf16[2048,1024]{1,0:T(8,128)(2,1)} %wv_h.1, bf16[1024,2048]{1,0:T(8,128)(2,1)} %wo_h.1, bf16[256,1024]{1,0:T(8,128)(2,1)} %cot_h.1), custom_call_target="tpu_custom_call" | custom-call | tf_op jit(solution)/shard_map/pallas_call | solution.py:581
  74.8 2.0 %shard_map.78 = (bf16[256,1024]{1,0:T(8,128)(2,1)}, bf16[256,1024]{1,0:T(8,128)(2,1)}) custom-call(bf16[256,1024]{1,0:T(8,128)(2,1)} %get-tuple-element.4.a, bf16[256,1024]{1,0:T(8,128)(2,1)} %get-tuple-element.5.b), custom_call_target="tpu_custom_call" | custom-call | tf_op jit(solution)/shard_map/pallas_call | solution.py:591

commit v4 on v3

--- a/solution.py
+++ b/solution.py
@@ -66,7 +66,7 @@
     M_TOK, M_COTC, M_COTH, M_COTF, M_MIXC, M_MIXH, M_INC, M_INH,
     M_Y, M_X1, M_X2, M_ZO, M_ZW, M_ZX, M_ZY,
     B_XA, B_Z, B_ZY, B_Y, M_LC, M_LH, N_MSG,
-) = (0, 2, 3, 5, 7, 11, 13, 17, 19, 22, 24, 25, 31, 34, 40, 43, 44, 56, 68, 71, 75, 77)
+) = (0, 2, 3, 5, 7, 11, 13, 17, 19, 22, 24, 25, 31, 34, 40, 43, 44, 56, 68, 74, 78, 80)
 
 
 def kernel(
@@ -431,32 +431,47 @@
             plane = plane + returned(plane_region(k, dx))
         return top, plane
 
-    lax.fori_loop(0, 8, in_early, 0)
     for i in range(4):
         s_mixc[i].wait_send()
 
     def in_piece(i):
+        lax.fori_loop(2 * i, 2 * i + 2, in_early, 0)
         c_send[i] = acc[pl.ds(TOK, TOK), cols(i)].astype(BF16)
         return send(M_INC + i, c_send.at[i], ic_recv.at[i], core)
 
-    s_inc = {i: in_piece(i) for i in (2, 3, 0, 1)}
+    def early_piece(i):
+        return head_piece(i, s_inc[2 + i], acc, ic_recv, M_INH, ih_send, ih_recv)
+
+    s_inc = {i: in_piece(i) for i in (2, 3)}
+    s_inh = [early_piece(0)]
+
+    def send_y(dx, plane):
+        gy_s[dx, 0] = plane[0:16].astype(BF16)
+        high = spread(plane[16:32])
+        gy_s[dx, 1] = high[0:16].astype(BF16)
+        gy_s[dx, 2] = high[16:32].astype(BF16)
+        return [
+            send(B_Y + 3 * dx + k - 1, gy_s.at[dx, k - 1], gy_r.at[dx, k - 1], ydev[k]) for k in (1, 2, 3)
+        ]
+
+    def add_y(dx, top):
+        for cp in b_y[dx]:
+            cp.wait_recv()
+        g4 = gy_r[dx, 0].astype(F32) + gy_r[dx, 1].astype(F32) + gy_r[dx, 2].astype(F32)
+        return top + spread(spread(g4))
+
+    b_y = {}
     top, plane = collect(1)
-    xa_s[pl.ds(0, 128), :] = (spread(top) + dS[pl.ds(0, 128), :]).astype(BF16)
-    xa_s[pl.ds(128, 32), :] = plane.astype(BF16)
+    b_y[1] = send_y(1, plane)
+    pf[pl.ds(0, 64), :] = top
+    top = add_y(1, pf[pl.ds(0, 64), :])
+    xa_s[...] = (spread(top) + dS[pl.ds(0, 128), :]).astype(BF16)
     b_xa = send(B_XA, xa_s, xa_r, xhi)
-    s_inh = [head_piece(i, s_inc[2 + i], acc, ic_recv, M_INH, ih_send, ih_recv) for i in (0, 1)]
+    s_inh.append(early_piece(1))
+    s_inc.update({i: in_piece(i) for i in (0, 1)})
     top, plane = collect(0)
-    pf[pl.ds(0, 64), :] = top
-    pf[pl.ds(64, 32), :] = plane
-
-    b_xa.wait_recv()
-    top = pf[pl.ds(0, 64), :]
-    plane = pf[pl.ds(64, 32), :] + xa_r[pl.ds(128, 32), :].astype(F32)
-    gy_s[0] = plane[0:16].astype(BF16)
-    high = spread(plane[16:32])
-    gy_s[1] = high[0:16].astype(BF16)
-    gy_s[2] = high[16:32].astype(BF16)
-    b_y = [send(B_Y + k - 1, gy_s.at[k - 1], gy_r.at[k - 1], ydev[k]) for k in (1, 2, 3)]
+    b_y[0] = send_y(0, plane)
+    pf[pl.ds(64, 64), :] = top
 
     for i in (0, 1):
         s_mixc[i].wait_recv()
@@ -464,11 +479,9 @@
         last_piece(i, macc, c_recv, h_recv)
     st_mix = load(out_b, mix_o)
 
-    for cp in b_y:
-        cp.wait_recv()
-    g4 = gy_r[0].astype(F32) + gy_r[1].astype(F32) + gy_r[2].astype(F32)
-    top = top + spread(spread(g4))
-    low = spread(top) + xa_r[pl.ds(0, 128), :].astype(F32)
+    low = spread(add_y(0, pf[pl.ds(64, 64), :]))
+    b_xa.wait_recv()
+    low = low + xa_r[...].astype(F32)
     low = low.astype(BF16)
     out_i = lax.broadcasted_iota(jnp.int32, (TOK, 64), 0)
     inp_i = lax.broadcasted_iota(jnp.int32, (TOK, 64), 1)
@@ -509,7 +522,7 @@
         cp.wait_send()
     for cp in s_tok + s_coth + s_cotf + s_inh + list(s_inc.values()) + [s_cotc, m_x2, b_xa]:
         cp.wait_send()
-    for cp in m_x1 + m_y + m_zo + m_zw + m_zx + m_zy + b_y + b_z[0] + b_z[1]:
+    for cp in m_x1 + m_y + m_zo + m_zw + m_zx + m_zy + b_y[0] + b_y[1] + b_z[0] + b_z[1]:
         cp.wait_send()
     st_in.wait()
 
@@ -539,7 +552,7 @@
         V((32, 2 * WID), BF16),
         V((3, 16, 2 * WID), BF16),
         V((ROWS, 2 * WID), BF16),
-        V((96, 2 * WID), F32),
+        V((128, 2 * WID), F32),
         V((8, 1024, 256), F32),
         V((5, 8, 8, 256), F32),
         V((8, 8, 256), F32),
@@ -565,10 +578,10 @@
         V((ROWS, 2 * WID), F32),
         V((2, ROWS, WID), BF16),
         V((2, ROWS, WID), BF16),
-        V((160, 2 * WID), BF16),
-        V((160, 2 * WID), BF16),
-        V((3, 16, 2 * WID), BF16),
-        V((3, 16, 2 * WID), BF16),
+        V((128, 2 * WID), BF16),
+        V((128, 2 * WID), BF16),
+        V((2, 3, 16, 2 * WID), BF16),
+        V((2, 3, 16, 2 * WID), BF16),
         V((2 * TOK, WID), BF16),
         V((2 * TOK, 2 * WID), BF16),
         V((TOK, HALF), BF16),

time: 77.1 us -> 75.3 us (0.977)
  Pallas kernels: 76.2 us -> 74.5 us
    pallas_call x1, Pallas kernels: 74.1 us -> 72.5 us  [per_device(): pl.pallas_call(kernel, out_shape=(out, out), in_specs=[any_spec] * 6, out...]
where the time goes in v4:
time: 75.3 us; the launch traced here: 75.2 us
  Pallas kernels  74.5 us (99%)
    pallas_call x1, Pallas kernels, per_device(): pl.pallas_call(kernel, out_shape=(out, out), in_specs=[any_spec] * 6, out...  72.5 us
    pallas_call x1, Pallas kernels, per_device(): pl.pallas_call(copy_out, grid=(2,), out_shape=(out, out), in_specs=[pl.Bl...  2.04 us

profile of v4, /device:TPU:1, one launch (start us, length us, event | category | flops | bytes accessed | tf_op | source)
XLA Modules:
  0.0 75.2 jit_solution(10462643335177907772)
XLA Ops:
  0.6 72.5 %shard_map.77 = (bf16[256,1024]{1,0:T(8,128)(2,1)}, bf16[256,1024]{1,0:T(8,128)(2,1)}) custom-call(bf16[256,2048]{1,0:T(8,128)(2,1)} %tok_h.1, bf16[2048,1024]{1,0:T(8,128)(2,1)} %wq_h.1, bf16[2048,1024]{1,0:T(8,128)(2,1)} %wk_h.1, bf16[2048,1024]{1,0:T(8,128)(2,1)} %wv_h.1, bf16[1024,2048]{1,0:T(8,128)(2,1)} %wo_h.1, bf16[256,1024]{1,0:T(8,128)(2,1)} %cot_h.1), custom_call_target="tpu_custom_call" | custom-call | tf_op jit(solution)/shard_map/pallas_call | solution.py:594
  73.1 2.0 %shard_map.78 = (bf16[256,1024]{1,0:T(8,128)(2,1)}, bf16[256,1024]{1,0:T(8,128)(2,1)}) custom-call(bf16[256,1024]{1,0:T(8,128)(2,1)} %get-tuple-element.4.a, bf16[256,1024]{1,0:T(8,128)(2,1)} %get-tuple-element.5.b), custom_call_target="tpu_custom_call" | custom-call | tf_op jit(solution)/shard_map/pallas_call | solution.py:604

commit v5 on v4

--- a/solution.py
+++ b/solution.py
@@ -143,11 +143,11 @@
 
     def kv_tiles(b):
         def body(j, _):
-            r = dot(tok[pl.ds(b * TOK, TOK), :], w[:, lanes(j, 256)]).astype(BF16)
-            kv[pl.ds(b * TOK, TOK), lanes(j, 256)] = r
+            r = dot(tok[pl.ds(b * TOK, TOK), :], w[:, lanes(j, 512)]).astype(BF16)
+            kv[pl.ds(b * TOK, TOK), lanes(j, 512)] = r
             return 0
 
-        lax.fori_loop(0, 4, body, 0)
+        lax.fori_loop(0, 2, body, 0)
 
     m_x1, m_zo, m_zx = [], [], []
 
@@ -254,7 +254,6 @@
     pass_x(0)
     each((score, 0))
     pass_x(1)
-    each((score, 1))
     m_x2.wait_recv()
     s_coth.append(send_cot(1))
     m_zy = [
@@ -264,7 +263,7 @@
 
     for cp in m_zo + m_zw:
         cp.wait_recv()
-    each((score, 2))
+    each((score, 1), (score, 2))
 
     for cp in m_zx:
         cp.wait_recv()
@@ -507,14 +506,14 @@
     for i in (0, 1):
         s_inc[i].wait_recv()
         s_inh[i].wait_recv()
+        acc[pl.ds(0, TOK), cols(i)] += ic_recv[i].astype(F32) + ih_recv[i].astype(F32)
+    st_in = []
+    for i in (0, 1):
         s_lc[i].wait_recv()
         s_lh[i].wait_recv()
         late = lacc[:, cols(i)] + lc_recv[i].astype(F32) + lh_recv[i].astype(F32)
-        out_b[:, cols(i)] = (
-            acc[pl.ds(0, TOK), cols(i)] + ic_recv[i].astype(F32) + ih_recv[i].astype(F32)
-            + dot(quarter, late.astype(BF16))
-        ).astype(BF16)
-    st_in = load(out_b, ing_o)
+        out_b[:, cols(i)] = (acc[pl.ds(0, TOK), cols(i)] + dot(quarter, late.astype(BF16))).astype(BF16)
+        st_in.append(load(out_b.at[:, cols(i)], ing_o.at[:, cols(i)]))
 
     for i in (0, 1):
         s_mixh[i].wait_send()
@@ -524,7 +523,8 @@
         cp.wait_send()
     for cp in m_x1 + m_y + m_zo + m_zw + m_zx + m_zy + b_y[0] + b_y[1] + b_z[0] + b_z[1]:
         cp.wait_send()
-    st_in.wait()
+    for cp in st_in:
+        cp.wait()
 
 
 def copy_out(a, b, a_o, b_o):

time: 75.3 us -> 75 us (level)
  no operation moved by 1% of the time
where the time goes in v5:
time: 75 us; the launch traced here: 74.8 us
  Pallas kernels  74.2 us (99%)
    pallas_call x1, Pallas kernels, per_device(): pl.pallas_call(kernel, out_shape=(out, out), in_specs=[any_spec] * 6, out...  72.2 us
    pallas_call x1, Pallas kernels, per_device(): pl.pallas_call(copy_out, grid=(2,), out_shape=(out, out), in_specs=[pl.Bl...  2.04 us

profile of v5, /device:TPU:1, one launch (start us, length us, event | category | flops | bytes accessed | tf_op | source)
XLA Modules:
  0.0 74.8 jit_solution(1694968110173070009)
XLA Ops:
  0.6 72.2 %shard_map.77 = (bf16[256,1024]{1,0:T(8,128)(2,1)}, bf16[256,1024]{1,0:T(8,128)(2,1)}) custom-call(bf16[256,2048]{1,0:T(8,128)(2,1)} %tok_h.1, bf16[2048,1024]{1,0:T(8,128)(2,1)} %wq_h.1, bf16[2048,1024]{1,0:T(8,128)(2,1)} %wk_h.1, bf16[2048,1024]{1,0:T(8,128)(2,1)} %wv_h.1, bf16[1024,2048]{1,0:T(8,128)(2,1)} %wo_h.1, bf16[256,1024]{1,0:T(8,128)(2,1)} %cot_h.1), custom_call_target="tpu_custom_call" | custom-call | tf_op jit(solution)/shard_map/pallas_call | solution.py:594
  72.8 2.0 %shard_map.78 = (bf16[256,1024]{1,0:T(8,128)(2,1)}, bf16[256,1024]{1,0:T(8,128)(2,1)}) custom-call(bf16[256,1024]{1,0:T(8,128)(2,1)} %get-tuple-element.4.a, bf16[256,1024]{1,0:T(8,128)(2,1)} %get-tuple-element.5.b), custom_call_target="tpu_custom_call" | custom-call | tf_op jit(solution)/shard_map/pallas_call | solution.py:604

commit v6 on v5

--- a/solution.py
+++ b/solution.py
@@ -299,9 +299,10 @@
         return pl.ds(i * 512, 512)
 
     def out_piece(i):
+        c_send[i] = dot(att[pl.ds(TOK, TOK), :], wo[:, cols(i)]).astype(BF16)
+        cp = send(M_MIXC + i, c_send.at[i], c_recv.at[i], core)
         macc[:, cols(i)] = dot(att[pl.ds(0, TOK), :], wo[:, cols(i)])
-        c_send[i] = dot(att[pl.ds(TOK, TOK), :], wo[:, cols(i)]).astype(BF16)
-        return send(M_MIXC + i, c_send.at[i], c_recv.at[i], core)
+        return cp
 
     def head_piece(i, cp, total, got, base, src, dst):
         cp.wait_recv()

time: 75 us -> 74.8 us (level)
  no operation moved by 1% of the time
where the time goes in v6:
time: 74.8 us; the launch traced here: 74.7 us
  Pallas kernels  74 us (99%)
    pallas_call x1, Pallas kernels, per_device(): pl.pallas_call(kernel, out_shape=(out, out), in_specs=[any_spec] * 6, out...  72 us
    pallas_call x1, Pallas kernels, per_device(): pl.pallas_call(copy_out, grid=(2,), out_shape=(out, out), in_specs=[pl.Bl...  2.04 us

profile of v6, /device:TPU:1, one launch (start us, length us, event | category | flops | bytes accessed | tf_op | source)
XLA Modules:
  0.0 74.7 jit_solution(13782635253391281448)
XLA Ops:
  0.6 72.0 %shard_map.77 = (bf16[256,1024]{1,0:T(8,128)(2,1)}, bf16[256,1024]{1,0:T(8,128)(2,1)}) custom-call(bf16[256,2048]{1,0:T(8,128)(2,1)} %tok_h.1, bf16[2048,1024]{1,0:T(8,128)(2,1)} %wq_h.1, bf16[2048,1024]{1,0:T(8,128)(2,1)} %wk_h.1, bf16[2048,1024]{1,0:T(8,128)(2,1)} %wv_h.1, bf16[1024,2048]{1,0:T(8,128)(2,1)} %wo_h.1, bf16[256,1024]{1,0:T(8,128)(2,1)} %cot_h.1), custom_call_target="tpu_custom_call" | custom-call | tf_op jit(solution)/shard_map/pallas_call | solution.py:595
  72.6 2.0 %shard_map.78 = (bf16[256,1024]{1,0:T(8,128)(2,1)}, bf16[256,1024]{1,0:T(8,128)(2,1)}) custom-call(bf16[256,1024]{1,0:T(8,128)(2,1)} %get-tuple-element.4.a, bf16[256,1024]{1,0:T(8,128)(2,1)} %get-tuple-element.5.b), custom_call_target="tpu_custom_call" | custom-call | tf_op jit(solution)/shard_map/pallas_call | solution.py:605
